TPU v7x, 256 devices: a whole 4x4x8 slice. The times are simulated.
256 devices in a mesh: head: 8 (over x, y_lo), inner: 8 (over z), outer: 4 (over y_hi, core).
Axes of the slice: x: 4, y: 4 (y_hi: 2, y_lo: 2; y = y_hi * 2 + y_lo), z: 8, core: 2. Of those that a mesh axis runs over, the one named last changes fastest.
Arguments:
- queries: bfloat16 [4096, 8192], P(('inner', 'outer'), 'head'), may hold values from -100 to 100
- keys: bfloat16 [4096, 1024], P(('inner', 'outer'), 'head'), may hold values from -4 to 4
- values: bfloat16 [4096, 1024], P(('inner', 'outer'), 'head'), may hold values from -6 to 6
- output_gradient: bfloat16 [4096, 8192], P(('inner', 'outer'), 'head'), may hold values from -6 to 6
- block_perm: int32 [64], replicated, may hold values from 0 to 63, as said below
- segment_ids: int32 [4096], replicated, may hold values from 0 to 3, as said below
Outputs:
- attended: bfloat16 [4096, 8192], P(('inner', 'outer'), 'head')
- query_grad: bfloat16 [4096, 8192], P(('inner', 'outer'), 'head')
- key_grad: bfloat16 [4096, 1024], P(('inner', 'outer'), 'head')
- value_grad: bfloat16 [4096, 1024], P(('inner', 'outer'), 'head')
Inputs may be any that keep to these rules, and one draw needn't show every extreme that they name: `block_perm`: each of 0 to 63 exactly once. `segment_ids`: document ids never fall along the rollout order.
All inputs are finite; a program needn't handle non-finite values.
Results may differ from a plain program's by a relative error of at most 0.039.
Values may be sent and summed in bfloat16 or wider, within the bound.
No kernel may reach another device: no remote copies, remote signals or barrier semaphores. Data moves between devices by JAX's collectives and lax.ppermute only.
A program may use at most 64 MiB of HBM per device.

v0:
```python
import math

import jax
import jax.numpy as jnp
from jax import lax
from jax.sharding import PartitionSpec as P

KEY_VALUE_HEADS = 8
HEAD_DIMENSION = 128


def on_device(queries, keys, values, output_gradient, block_perm, segment_ids):
    rows = queries.shape[0]
    heads_per_shard = queries.shape[1] // HEAD_DIMENSION
    kv_dev = keys.shape[1] // HEAD_DIMENSION
    groups = lax.axis_size("head")
    queries_per_group = heads_per_shard // KEY_VALUE_HEADS
    seq_len = segment_ids.shape[0]
    blocks = block_perm.shape[0]
    block = seq_len // blocks
    span = min(seq_len, 4 * rows)
    scale = 1.0 / math.sqrt(HEAD_DIMENSION)
    width = kv_dev * HEAD_DIMENSION

    def regroup(table):
        return table.reshape(rows, queries_per_group, groups, kv_dev, HEAD_DIMENSION)

    q_in, grad_in = (
        lax.all_to_all(regroup(queries), "head", split_axis=2, concat_axis=2, tiled=True),
        lax.all_to_all(regroup(output_gradient), "head", split_axis=2, concat_axis=2, tiled=True),
    )
    query_head_rows = q_in.reshape(rows, queries_per_group * groups, kv_dev, HEAD_DIMENSION)
    grad_heads = grad_in.reshape(rows, queries_per_group * groups, kv_dev, HEAD_DIMENSION)
    positions = (block_perm[:, None] * block + jnp.arange(block, dtype=jnp.int32)[None, :]).reshape(
        seq_len
    )
    documents = segment_ids.reshape(blocks, block)[block_perm].reshape(seq_len)
    first = lax.axis_index(("inner", "outer")) * rows
    q_pos = lax.dynamic_slice_in_dim(positions, first, rows)
    q_doc = lax.dynamic_slice_in_dim(documents, first, rows)
    stat_shape = (rows, queries_per_group * groups, kv_dev)
    zero_acc = jnp.zeros((rows, queries_per_group * groups, kv_dev, HEAD_DIMENSION), jnp.float32)

    def scores(key_piece, start):
        count = key_piece.shape[0]
        key_heads = key_piece.reshape(count, kv_dev, HEAD_DIMENSION)
        logits = (
            jnp.einsum(
                "tgud,pud->tgup", query_head_rows, key_heads, preferred_element_type=jnp.float32
            )
            * scale
        )
        k_pos = lax.dynamic_slice_in_dim(positions, start, count)
        k_doc = lax.dynamic_slice_in_dim(documents, start, count)
        allowed = (k_pos[None, :] <= q_pos[:, None]) & (k_doc[None, :] == q_doc[:, None])
        return (logits, allowed[:, None, None, :])

    def bounded(stepfn, carry, pieces, start):
        count = pieces[0].shape[0]

        def inner(index, state):
            begin = index * span
            parts = tuple((lax.dynamic_slice_in_dim(table, begin, span, 0) for table in pieces))
            return stepfn(state, parts, start + begin)

        return lax.fori_loop(0, count // span, inner, carry)

    def add_stats(carry, pieces, start):
        top, total = carry
        logits, allowed = scores(pieces[0], start)
        newtop = jnp.maximum(top, jnp.max(jnp.where(allowed, logits, -1e30), axis=-1))
        fresh = jnp.sum(jnp.where(allowed, jnp.exp(logits - newtop[..., None]), 0.0), axis=-1)
        return (newtop, total * jnp.exp(top - newtop) + fresh)

    def weights(pieces, start):
        logits, allowed = scores(pieces[0], start)
        return jnp.where(allowed, jnp.exp(logits - lse[..., None]), 0.0)

    def add_out(acc, pieces, start):
        probs = weights(pieces, start).astype(jnp.bfloat16)
        value_heads = pieces[1].reshape(-1, kv_dev, HEAD_DIMENSION)
        return acc + jnp.einsum(
            "tgup,pud->tgud", probs, value_heads, preferred_element_type=jnp.float32
        )

    def prob_pair(pieces, start):
        probs = weights(pieces, start)
        value_heads = pieces[1].reshape(-1, kv_dev, HEAD_DIMENSION)
        dprobs = jnp.einsum(
            "tgud,pud->tgup", grad_heads, value_heads, preferred_element_type=jnp.float32
        )
        dscore = (probs * (dprobs - delta[..., None])).astype(jnp.bfloat16)
        return (probs, dscore)

    def add_back(carry, pieces, start):
        dq_acc, term_all = carry
        count = pieces[0].shape[0]
        probs, dscore = prob_pair(pieces, start)
        key_heads = pieces[0].reshape(count, kv_dev, HEAD_DIMENSION)
        dq_acc = dq_acc + jnp.einsum(
            "tgup,pud->tgud", dscore, key_heads, preferred_element_type=jnp.float32
        )
        value_gradient = jnp.einsum(
            "tgup,tgud->pud",
            probs.astype(jnp.bfloat16),
            grad_heads,
            preferred_element_type=jnp.float32,
        )
        key_gradient = (
            jnp.einsum(
                "tgup,tgud->pud", dscore, query_head_rows, preferred_element_type=jnp.float32
            )
            * scale
        )
        fresh_rows = jnp.concatenate(
            [key_gradient.reshape(count, width), value_gradient.reshape(count, width)], axis=1
        )
        term_all = lax.dynamic_update_slice_in_dim(term_all, fresh_rows, start, 0)
        return (dq_acc, term_all)

    init = (jnp.full(stat_shape, -1e30, jnp.float32), jnp.zeros(stat_shape, jnp.float32))
    kv_whole = (
        lax.all_gather(keys, ("inner", "outer"), axis=0, tiled=True),
        lax.all_gather(values, ("inner", "outer"), axis=0, tiled=True),
    )
    top, total = bounded(add_stats, init, kv_whole, 0)
    lse = top + jnp.log(total)
    out_acc = bounded(add_out, zero_acc, kv_whole, 0)
    attended = out_acc.astype(jnp.bfloat16)
    delta = jnp.sum(grad_heads.astype(jnp.float32) * attended.astype(jnp.float32), axis=-1)
    back_init = (zero_acc, jnp.zeros((seq_len, 2 * width), jnp.float32))
    dq_acc, term_all = bounded(add_back, back_init, kv_whole, 0)
    grads = lax.psum_scatter(term_all, ("inner", "outer"), scatter_dimension=0, tiled=True)
    qgrad = (dq_acc * scale).astype(jnp.bfloat16)
    back_out, back_dq = (
        lax.all_to_all(regroup(attended), "head", split_axis=2, concat_axis=2, tiled=True),
        lax.all_to_all(regroup(qgrad), "head", split_axis=2, concat_axis=2, tiled=True),
    )
    return (
        back_out.reshape(rows, heads_per_shard * HEAD_DIMENSION),
        back_dq.reshape(rows, heads_per_shard * HEAD_DIMENSION),
        grads[:, :width].astype(jnp.bfloat16),
        grads[:, width:].astype(jnp.bfloat16),
    )


def solution(mesh):
    return jax.shard_map(
        on_device,
        mesh=mesh,
        in_specs=(
            P(("inner", "outer"), "head"),
            P(("inner", "outer"), "head"),
            P(("inner", "outer"), "head"),
            P(("inner", "outer"), "head"),
            P(),
            P(),
        ),
        out_specs=(
            P(("inner", "outer"), "head"),
            P(("inner", "outer"), "head"),
            P(("inner", "outer"), "head"),
            P(("inner", "outer"), "head"),
        ),
        check_vma=False,
    )
```

profile of v0, /device:TPU:1, one launch (start us, length us, event | category | flops | bytes accessed | tf_op | source)
XLA Modules:
  0.0 370.5 jit_solution(14812001790108433857)
XLA Ops:
  7.9 1.8 copy.32
  9.7 5.9 %all-to-all-start = ((bf16[128,1,8,1,128]{0,4,3,1,2:T(8,128)(2,1)}), bf16[128,1,8,1,128]{0,4,3,1,2:T(8,128)(2,1)S(1)}, u32[]{:S(2)}, u32[]{:S(2)}) async-start(bf16[128,1,8,1,128]{0,4,3,1,2:T(8,128)(2,1)} %bitcast), calls=%async_computation | async-start | bytes 524288 | tf_op jit(solution)/shard_map/all_to_all | solution.py:29
  18.8 1.8 copy.36
  21.5 4.2 %all-to-all-start.2 = ((bf16[128,1,8,1,128]{0,4,3,1,2:T(8,128)(2,1)}), bf16[128,1,8,1,128]{0,4,3,1,2:T(8,128)(2,1)S(1)}, u32[]{:S(2)}, u32[]{:S(2)}) async-start(bf16[128,1,8,1,128]{0,4,3,1,2:T(8,128)(2,1)} %bitcast.4), calls=%async_computation.2 | async-start | bytes 524288 | tf_op jit(solution)/shard_map/all_to_all | solution.py:30
  25.9 66.9 %all-gather.5.cloned.1.call-done = bf16[4096,128]{1,0:T(8,128)(2,1)} async-done(((bf16[128,128]{1,0:T(8,128)(2,1)}), bf16[4096,128]{1,0:T(8,128)(2,1)}) %all-gather.5.cloned.1.call-update) | async-done | bytes 1048592 | tf_op jit(solution)/shard_map/all_gather | solution.py:123
  92.8 17.9 %while.46 = (s32[]{:T(128)}, f32[128,8,1]{0,1,2:T(8,128)S(1)}, f32[128,8,1]{0,1,2:T(8,128)S(1)}, s32[4096]{0:T(1024)S(1)}, s32[128]{0:T(128)S(1)}, /*index=5*/s3...) while((s32[]{:T(128)}, f32[128,8,1]{0,1,2:T(8,128)S(1)}, ...), condition=%wide.region_3.4_spmd.clone, body=%wide.region_0.3_spmd.clone.sunk | while | flops 138089472 | bytes 4850890 | solution.py:66
  110.8 59.3 %all-gather.3.cloned.1.call-done = bf16[4096,128]{1,0:T(8,128)(2,1)} async-done(((bf16[128,128]{1,0:T(8,128)(2,1)}), bf16[4096,128]{1,0:T(8,128)(2,1)}) %all-gather.3.cloned.1.call-update) | async-done | bytes 1048592 | tf_op jit(solution)/shard_map/all_gather | solution.py:124
  170.1 17.0 %while.47 = (s32[]{:T(128)}, f32[128,8,1,128]{0,3,1,2:T(8,128)S(1)}, bf16[4096,128]{1,0:T(8,128)(2,1)}, s32[4096]{0:T(1024)S(1)}, s32[128]{0:T(128)S(1)}, /*inde...) while((s32[]{:T(128)}, ...), condition=%wide.region_5.6_spmd.clone, body=%wide.region_4.5_spmd.clone.sunk | while | flops 270991360 | bytes 1723084 | solution.py:66
  170.4 1.7 fusion.77
  172.6 1.7 fusion.77
  174.7 1.7 fusion.77
  176.8 1.7 fusion.77
  178.9 1.7 fusion.77
  181.0 1.7 fusion.77
  183.2 1.7 fusion.77
  185.3 1.7 fusion.77
  187.8 2.2 broadcast_in_dim.152.clone
  190.0 52.3 %while.48 = (s32[]{:T(128)}, f32[128,8,1,128]{0,3,1,2:T(8,128)S(1)}, f32[4096,256]{1,0:T(8,128)}, bf16[4096,128]{1,0:T(8,128)(2,1)}, s32[4096]{0:T(1024)S(1)}, /...) while((s32[]{:T(128)}, ...), condition=%wide.region_8.9_spmd.clone, body=%wide.region_7.8_spmd.clone.sunk | while | flops 675414016 | bytes 15750389 | solution.py:66
  229.6 1.5 bitcast_select_fusion.4
  242.4 4.0 %all-to-all-start.1 = ((bf16[128,1,8,1,128]{0,4,3,1,2:T(8,128)(2,1)}), bf16[128,1,8,1,128]{0,4,3,1,2:T(8,128)(2,1)S(1)}, u32[]{:S(2)}, u32[]{:S(2)}) async-start(bf16[128,1,8,1,128]{0,4,3,1,2:T(8,128)(2,1)} %get-tuple-element.762), calls=%async_computation.1 | async-start | bytes 524288 | tf_op jit(solution)/shard_map/all_to_all | solution.py:136
  247.1 5.3 %all-to-all-done.1 = bf16[128,1,8,1,128]{0,4,3,1,2:T(8,128)(2,1)S(1)} async-done(((bf16[128,1,8,1,128]{0,4,3,1,2:T(8,128)(2,1)}), bf16[128,1,8,1,128]{0,4,3,1,2:T(8,128)(2,1)S(1)}, u32[]{:S(2)}, u32[]{:S(2)}) %all-to-all-start.1) | async-done | bytes 262176 | tf_op jit(solution)/shard_map/all_to_all | solution.py:136
  252.4 3.5 all-to-all-start.3
  256.7 5.0 %all-to-all-done.3 = bf16[128,1,8,1,128]{0,4,3,1,2:T(8,128)(2,1)S(1)} async-done(((bf16[128,1,8,1,128]{0,4,3,1,2:T(8,128)(2,1)}), bf16[128,1,8,1,128]{0,4,3,1,2:T(8,128)(2,1)S(1)}, u32[]{:S(2)}, u32[]{:S(2)}) %all-to-all-start.3) | async-done | bytes 262176 | tf_op jit(solution)/shard_map/all_to_all | solution.py:137
  262.5 99.9 %reduce-scatter.2.cloned.1.call-done = f32[128,256]{1,0:T(8,128)} async-done(((f32[4096,256]{1,0:T(8,128)}), f32[128,256]{1,0:T(8,128)}) %reduce-scatter.2.cloned.1.call-update) | async-done | bytes 131088 | tf_op jit(solution)/shard_map/reduce_scatter | solution.py:133
  (204 shorter events, 80.4 us)
Async XLA Ops:
  7.2 85.7 %all-gather.5.cloned.1.call-start = ((), (), s32[]{:S(2)}) async-start(), calls=%async_computation.6 | async-start | bytes 1081344 | tf_op jit(solution)/shard_map/all_gather | solution.py:123
  9.7 11.8 %all-to-all-start = ((bf16[128,1,8,1,128]{0,4,3,1,2:T(8,128)(2,1)}), bf16[128,1,8,1,128]{0,4,3,1,2:T(8,128)(2,1)S(1)}, u32[]{:S(2)}, u32[]{:S(2)}) async-start(bf16[128,1,8,1,128]{0,4,3,1,2:T(8,128)(2,1)} %bitcast), calls=%async_computation | async-start | bytes 524288 | tf_op jit(solution)/shard_map/all_to_all | solution.py:29
  15.6 154.5 %all-gather.3.cloned.1.call-start = ((), (), s32[]{:S(2)}) async-start(), calls=%async_computation.5 | async-start | bytes 1081344 | tf_op jit(solution)/shard_map/all_gather | solution.py:124
  21.5 165.6 %all-to-all-start.2 = ((bf16[128,1,8,1,128]{0,4,3,1,2:T(8,128)(2,1)}), bf16[128,1,8,1,128]{0,4,3,1,2:T(8,128)(2,1)S(1)}, u32[]{:S(2)}, u32[]{:S(2)}) async-start(bf16[128,1,8,1,128]{0,4,3,1,2:T(8,128)(2,1)} %bitcast.4), calls=%async_computation.2 | async-start | bytes 524288 | tf_op jit(solution)/shard_map/all_to_all | solution.py:30
  25.7 336.8 %reduce-scatter.2.cloned.1.call-start = ((), (), s32[]{:S(2)}) async-start(), calls=%async_computation.7 | async-start | bytes 4325376 | tf_op jit(solution)/shard_map/reduce_scatter | solution.py:133
  242.4 10.0 %all-to-all-start.1 = ((bf16[128,1,8,1,128]{0,4,3,1,2:T(8,128)(2,1)}), bf16[128,1,8,1,128]{0,4,3,1,2:T(8,128)(2,1)S(1)}, u32[]{:S(2)}, u32[]{:S(2)}) async-start(bf16[128,1,8,1,128]{0,4,3,1,2:T(8,128)(2,1)} %get-tuple-element.762), calls=%async_computation.1 | async-start | bytes 524288 | tf_op jit(solution)/shard_map/all_to_all | solution.py:136
  252.4 9.3 %all-to-all-start.3 = ((bf16[128,1,8,1,128]{0,4,3,1,2:T(8,128)(2,1)}), bf16[128,1,8,1,128]{0,4,3,1,2:T(8,128)(2,1)S(1)}, u32[]{:S(2)}, u32[]{:S(2)}) async-start(bf16[128,1,8,1,128]{0,4,3,1,2:T(8,128)(2,1)} %fusion.49), calls=%async_computation.3 | async-start | bytes 524288 | tf_op jit(solution)/shard_map/all_to_all | solution.py:137
Sparse Core Ops, SparseCore 0:
  10.8 82.0 all-gather.4
  95.6 74.3 all-gather.2
  242.5 119.9 reduce-scatter.1
where the time goes:
time: 375 us; the launch traced here: 371 us
  waiting for transfers between devices  239 us (64%)
  matrix products  65.1 us (17%)
  local copies, waits for them, and re-layouts  22 us (6%)
  starting transfers between devices  17.7 us (5%)
  between operations  13.8 us (4%)
  other arithmetic  12 us (3%)
    reduce_scatter x1, waiting for transfers between devices, on_device(): lax.psum_scatter(term_all, ('inner', 'outer'), scatter_dimension=0, tiled...  99.9 us
    all_gather x1, waiting for transfers between devices, on_device(): lax.all_gather(keys, ('inner', 'outer'), axis=0, tiled=True)  66.9 us
    all_gather x1, waiting for transfers between devices, on_device(): lax.all_gather(values, ('inner', 'outer'), axis=0, tiled=True)  59.3 us
    dot_general x16, matrix products, scores(): jnp.einsum('tgud,pud->tgup', query_head_rows, key_heads, preferred_elemen...  22.6 us
    dot_general x8, matrix products, add_out(): jnp.einsum('tgup,pud->tgud', probs, value_heads, preferred_element_type=j...  13.8 us
    dot_general x8, matrix products, prob_pair(): jnp.einsum('tgud,pud->tgup', grad_heads, value_heads, preferred_element_t...  10.7 us
    dot_general x8, matrix products, add_back(): jnp.einsum('tgup,pud->tgud', dscore, key_heads, preferred_element_type=jn...  10.5 us
    dynamic_update_slice x16, local copies, waits for them, and re-layouts, add_back(): term_all = lax.dynamic_update_slice_in_dim(term_all, fresh_rows, start, 0)  8.34 us
  transfers between devices with their start and end apart: 7, of which 6 were waited for; matrix products, arithmetic and copies ran while one was open for 12% of the time, Pallas kernels for 0%

commit v1 on v0

v1 whole, which is shorter than its diff:
```python
import functools
import math

import jax
import jax.numpy as jnp
from jax import lax
from jax.experimental import pallas as pl
from jax.experimental.pallas import tpu as pltpu
from jax.sharding import PartitionSpec as P

HEAD = 128
GROUP = 8
BLOCK = 64
TILE = 4 * BLOCK
LANES = GROUP * BLOCK
CALL = 16
SCALE = 1.0 / math.sqrt(HEAD)
SCALE2 = SCALE * math.log2(math.e)
LOW = -1e30
NT = (((1,), (1,)), ((), ()))
TN = (((0,), (0,)), ((), ()))
NN = (((1,), (0,)), ((), ()))
F32, BF16 = jnp.float32, jnp.bfloat16


def mm(a, b, dims):
    return lax.dot_general(a, b, dims, preferred_element_type=F32)


def blocks_of(kinds, refs, meta):
    z, outer = meta[0], meta[1]
    core = lax.rem(outer, 2)
    for (side, steps), ref in zip(kinds, refs, strict=True):
        sign = (1 - 2 * core) * (1 if side == "near" else -1)
        chunk = lax.rem(z - sign * steps + 8, 8)
        base = outer if side == "near" else outer + 1 - 2 * core
        twin = base + 1 - 2 * lax.rem(base, 2)
        shards = [base, lax.rem(base + 2, 4), twin, lax.rem(twin + 2, 4)]
        for i in range(ref.shape[0]):
            for b in range(2):
                yield ref, i, b * BLOCK, chunk * 8 + shards[i] * 2 + b


def limits(perm, meta, qb):
    lane = lax.rem(lax.broadcasted_iota(jnp.int32, (1, LANES), 1), BLOCK)
    block = perm[meta[0] * 8 + meta[1] * 2 + qb]
    first = block * BLOCK
    qpos = first + lane
    low = jnp.zeros_like(qpos)
    low_first = jnp.int32(0)
    for d in range(3):
        start = meta[2 + d]
        low = jnp.where(start <= qpos, jnp.maximum(low, start), low)
        low_first = jnp.where(start <= first, jnp.maximum(low_first, start), low_first)
    return qpos, low, low_first // BLOCK, block


def pick(perm, found, lowest, highest, k_s, v_s, pos_s, slot_s):
    n = jnp.int32(0)
    for i, (ref, shard, row, stored) in enumerate(found):
        at = pl.ds(pl.multiple_of(n * BLOCK, BLOCK), BLOCK)
        k_s[at, :] = ref[shard, 0, row : row + BLOCK, :]
        v_s[at, :] = ref[shard, 1, row : row + BLOCK, :]
        position = perm[stored]
        pos_s[n] = position
        slot_s[n] = i
        n = n + jnp.where((position >= lowest) & (position <= highest), 1, 0)
    for j in range(3):
        at = pl.ds(pl.multiple_of((n + j) * BLOCK, BLOCK), BLOCK)
        k_s[at, :] = jnp.zeros((BLOCK, HEAD), BF16)
        v_s[at, :] = jnp.zeros((BLOCK, HEAD), BF16)
        pos_s[n + j] = 1 << 14
        slot_s[n + j] = CALL
    return (n + 3) // 4


def tile(t):
    return pl.ds(pl.multiple_of(t * TILE, TILE), TILE)


def masked_scores(t, q, qpos, low, k_s, pos_s):
    row = lax.broadcasted_iota(jnp.int32, (BLOCK, 1), 0)
    kpos = jnp.concatenate([pos_s[4 * t + j] * BLOCK + row for j in range(4)], axis=0)
    return jnp.where((kpos <= qpos) & (kpos >= low), mm(k_s[tile(t), :], q, NT), LOW)


def heads_of(qd, which, qb):
    return jnp.concatenate([qd[i, which, qb * BLOCK : (qb + 1) * BLOCK, :] for i in range(GROUP)], axis=0)


def eights(x):
    return x.reshape(TILE // 8, 8, LANES)


def forward_kernel(kinds, first, last, *refs):
    perm, meta, qd, *refs = refs
    pieces, refs = refs[: len(kinds)], refs[len(kinds) :]
    if not first:
        stat_in, ot_in, *refs = refs
    stat, ot, k_s, v_s, s_s, pos_s, slot_s, *work = refs
    found = list(blocks_of(kinds, pieces, meta))
    for qb in range(2):
        q = heads_of(qd, 0, qb)
        qpos, low, lowest, highest = limits(perm, meta, qb)
        tiles = pick(perm, found, lowest, highest, k_s, v_s, pos_s, slot_s)

        def scores(t, top):
            s = masked_scores(t, q, qpos, low, k_s, pos_s)
            s_s[tile(t), :] = s
            return jnp.maximum(top, jnp.max(eights(s), axis=0))

        before = jnp.full((8, LANES), LOW, F32) if first else stat_in[qb, 0]
        top = lax.fori_loop(0, tiles, scores, before)
        top = jnp.max(top, axis=0, keepdims=True)
        acc = work[0] if last else ot.at[qb]
        if first:
            acc[...] = jnp.zeros((HEAD, LANES), F32)
            total = jnp.zeros((8, LANES), F32)
        else:
            keep = jnp.exp2((before[:1] - top) * SCALE2)
            acc[...] = ot_in[qb] * keep
            total = stat_in[qb, 1] * keep

        def sums(t, total):
            p = jnp.exp2((s_s[tile(t), :] - top) * SCALE2)
            acc[...] += mm(v_s[tile(t), :], p.astype(BF16), TN)
            return total + jnp.sum(eights(p), axis=0)

        total = lax.fori_loop(0, tiles, sums, total)
        if not last:
            stat[qb, 0] = jnp.broadcast_to(top, (8, LANES))
            stat[qb, 1] = total
            continue
        total = jnp.sum(total, axis=0, keepdims=True)
        out_t = acc[...] * (1.0 / total)
        out = out_t.T.astype(BF16)
        for i in range(GROUP):
            ot[i, qb * BLOCK : (qb + 1) * BLOCK, :] = out[i * BLOCK : (i + 1) * BLOCK, :]
        grad_t = heads_of(qd, 1, qb).astype(F32).T
        delta = jnp.sum(grad_t * out_t.astype(BF16).astype(F32), axis=0, keepdims=True)
        stat[qb, 0] = jnp.broadcast_to(top * SCALE2 + jnp.log2(total), (8, LANES))
        stat[qb, 1] = jnp.broadcast_to(delta, (8, LANES))


def backward_kernel(kinds, first, last, *refs):
    perm, meta, qd, stat, *refs = refs
    pieces, refs = refs[: len(kinds)], refs[len(kinds) :]
    if not first:
        dqt_in, *refs = refs
    if last:
        out, *refs = refs
    grads, refs = refs[: len(kinds)], refs[len(kinds) :]
    dq, k_s, v_s, dk_s, dv_s, pos_s, slot_s, *work = refs
    found = list(blocks_of(kinds, pieces, meta))
    dk_s[...] = jnp.zeros_like(dk_s)
    dv_s[...] = jnp.zeros_like(dv_s)
    for qb in range(2):
        q, do = heads_of(qd, 0, qb), heads_of(qd, 1, qb)
        qpos, low, lowest, highest = limits(perm, meta, qb)
        tiles = pick(perm, found, lowest, highest, k_s, v_s, pos_s, slot_s)
        lse, delta = stat[qb, 0, :1, :], stat[qb, 1, :1, :]
        acc = work[0] if last else dq.at[qb]
        acc[...] = jnp.zeros((HEAD, LANES), F32) if first else dqt_in[qb]

        def step(t, carry):
            p = jnp.exp2(masked_scores(t, q, qpos, low, k_s, pos_s) * SCALE2 - lse)
            dp = mm(v_s[tile(t), :], do, NT)
            ds = (p * (dp - delta)).astype(BF16)
            dv = mm(p.astype(BF16), do, NN)
            dk = mm(ds, q, NN)
            acc[...] += mm(k_s[tile(t), :], ds, TN)
            for j in range(4):
                at = pl.ds(pl.multiple_of(slot_s[4 * t + j] * BLOCK, BLOCK), BLOCK)
                dk_s[at, :] += dk[j * BLOCK : (j + 1) * BLOCK, :]
                dv_s[at, :] += dv[j * BLOCK : (j + 1) * BLOCK, :]
            return carry

        lax.fori_loop(0, tiles, step, 0)
        if last:
            done = (acc[...] * SCALE).T.astype(BF16)
            for i in range(GROUP):
                rows = slice(qb * BLOCK, (qb + 1) * BLOCK)
                dq[i, 0, rows, :] = out[i, rows, :]
                dq[i, 1, rows, :] = done[i * BLOCK : (i + 1) * BLOCK, :]
    n = 0
    for grad in grads:
        for i in range(grad.shape[0]):
            for b in range(2):
                at, rows = slice(n * BLOCK, (n + 1) * BLOCK), slice(b * BLOCK, (b + 1) * BLOCK)
                grad[i, 0, rows, :] = (dk_s[at, :] * SCALE).astype(BF16)
                grad[i, 1, rows, :] = dv_s[at, :].astype(BF16)
                n += 1


VMEM = pl.BlockSpec(memory_space=pltpu.VMEM)
SMEM = pl.BlockSpec(memory_space=pltpu.SMEM)
STAT = jax.ShapeDtypeStruct((2, 2, 8, LANES), F32)
WIDE = jax.ShapeDtypeStruct((2, HEAD, LANES), F32)
PICKED = [pltpu.VMEM(((CALL + 4) * BLOCK, HEAD), BF16)] * 2
LISTS = [pltpu.SMEM((CALL + 4,), jnp.int32)] * 2


def call(kernel, operands, outs, scratch, flops):
    return pl.pallas_call(
        kernel,
        out_shape=outs,
        in_specs=[SMEM, SMEM] + [VMEM] * (len(operands) - 2),
        out_specs=[VMEM] * len(outs),
        scratch_shapes=scratch,
        compiler_params=pltpu.CompilerParams(vmem_limit_bytes=20 * 1024 * 1024),
        cost_estimate=pl.CostEstimate(flops=flops, bytes_accessed=2 * 10**6, transcendentals=10**6),
    )(*operands)


def forward(perm, meta, qd, kinds, pieces, state, last):
    first = state is None
    outs = [STAT, jax.ShapeDtypeStruct((GROUP, 128, HEAD), BF16) if last else WIDE]
    scratch = PICKED + [pltpu.VMEM(((CALL + 4) * BLOCK, LANES), F32)] + LISTS
    scratch += [pltpu.VMEM((HEAD, LANES), F32)] if last else []
    kernel = functools.partial(forward_kernel, kinds, first, last)
    return call(kernel, [perm, meta, qd, *pieces, *(state or [])], outs, scratch, 5 * 10**8)


def backward(perm, meta, qd, stat, kinds, pieces, dqt, out):
    first, last = dqt is None, out is not None
    outs = [jax.ShapeDtypeStruct(p.shape, BF16) for p in pieces]
    outs.append(jax.ShapeDtypeStruct((GROUP, 2, 128, HEAD), BF16) if last else WIDE)
    scratch = PICKED + [pltpu.VMEM(((CALL + 1) * BLOCK, HEAD), F32)] * 2 + LISTS
    scratch += [pltpu.VMEM((HEAD, LANES), F32)] if last else []
    operands = [perm, meta, qd, stat, *pieces] + ([] if first else [dqt]) + ([out] if last else [])
    return call(functools.partial(backward_kernel, kinds, first, last), operands, outs, scratch, 10**9)


def outer_perm(move):
    pairs = []
    for z in range(8):
        for y in range(2):
            for c in range(2):
                z2, y2, c2 = move(z, y, c)
                pairs.append((z * 4 + y * 2 + c, (z2 % 8) * 4 + y2 * 2 + c2))
    return pairs


AXES = ("inner", "outer")
CORE = outer_perm(lambda z, y, c: (z, y, 1 - c))
TWIN = outer_perm(lambda z, y, c: (z, 1 - y, c))
CROSS = outer_perm(lambda z, y, c: (z, 1 - y, 1 - c))
ONWARD = outer_perm(lambda z, y, c: (z + 1 - 2 * c, y, c))
HOMEWARD = outer_perm(lambda z, y, c: (z - 1 + 2 * c, y, c))


def send(x, pairs):
    return lax.ppermute(x, AXES, pairs)


def after(*values):
    return lax.optimization_barrier(values)


def total32(*terms):
    return sum(t.astype(F32) for t in terms)


def add(*terms):
    return total32(*terms).astype(BF16)


def on_device(queries, keys, values, output_gradient, block_perm, segment_ids):
    rows = queries.shape[0]
    kv = jnp.stack([keys, values])
    own = jnp.stack([kv, *(send(kv, pairs) for pairs in (TWIN, CORE, CROSS))])
    qd = jnp.stack([queries.reshape(rows, GROUP, HEAD), output_gradient.reshape(rows, GROUP, HEAD)])
    qd = lax.all_to_all(jnp.transpose(qd, (2, 0, 1, 3)), "head", 0, 0, tiled=True)
    starts = jnp.sum(segment_ids[None, :] < jnp.arange(1, 4, dtype=jnp.int32)[:, None], axis=1)
    place = jnp.stack([lax.axis_index("inner"), lax.axis_index("outer")])
    meta = jnp.concatenate([place.astype(jnp.int32), starts.astype(jnp.int32)])

    run = functools.partial(forward, block_perm, meta, qd)
    near1 = send(own, ONWARD)
    calls = [((("near", 0), ("near", 1)), (own, near1))]
    near2 = send(near1, ONWARD)
    far1 = send(near1, CORE)
    state = run(*calls[0], None, False)
    calls.append(((("far", 1), ("near", 2)), (far1, near2)))
    near3 = send(near2, ONWARD)
    far2 = send(near2, CORE)
    near3, *state = after(near3, *state)
    state = run(*calls[1], state, False)
    calls.append(((("far", 2), ("near", 3)), (far2, near3)))
    near4 = send(near3[:2], ONWARD)
    far3 = send(near3, CORE)
    state = run(*calls[2], state, False)
    near4, *state = after(near4, *state)
    far4 = send(near4, CORE)
    calls.append(((("far", 3), ("near", 4), ("far", 4)), (far3, near4, far4)))
    stat, out = run(*calls[3], state, True)

    run = functools.partial(backward, block_perm, meta, qd, stat)
    far3, near4, far4, dqt = run(*calls[3], None, None)
    far2, near3, dqt = run(*calls[2], dqt, None)
    moving = send(add(near4, send(far4, CORE)), HOMEWARD)
    far1, near2, dqt = run(*calls[1], dqt, None)
    moving = jnp.concatenate([moving, jnp.zeros_like(moving)])
    moving = send(add(near3, send(far3, CORE), moving), HOMEWARD)
    own_grad, near1, back = run(*calls[0], dqt, out)
    back = lax.all_to_all(back, "head", 0, 0, tiled=True)
    moving = send(add(near2, send(far2, CORE), moving), HOMEWARD)
    moving = send(add(near1, send(far1, CORE), moving), HOMEWARD)
    total = total32(own_grad, moving)
    sent = total.astype(BF16)
    total = total[0] + total32(*(send(sent[i], pairs) for i, pairs in ((1, TWIN), (2, CORE), (3, CROSS))))
    total = total.astype(BF16)
    back = jnp.transpose(back, (1, 2, 0, 3)).reshape(2, rows, GROUP * HEAD)
    return back[0], back[1], total[0], total[1]


def solution(mesh):
    spec = P(("inner", "outer"), "head")
    return jax.shard_map(
        on_device,
        mesh=mesh,
        in_specs=(spec, spec, spec, spec, P(), P()),
        out_specs=(spec, spec, spec, spec),
        check_vma=False,
    )
```

time: 375 us -> 92.7 us (0.25)
  waiting for transfers between devices: 239 us -> 22.2 us
  matrix products: 65.1 us -> 0 us
  starting transfers between devices: 17.7 us -> 43.4 us
  Pallas kernels: 0 us -> 18.6 us
  local copies, waits for them, and re-layouts: 22 us -> 4.23 us
  between operations: 13.8 us -> 0.92 us
  other arithmetic: 12 us -> 2.42 us
    all_gather x2 -> x0, waiting for transfers between devices: 126 us -> none  [the longest x1 66.9 us: on_device(): lax.all_gather(keys, ('inner', 'outer'), axis=0, tiled=True)]
    reduce_scatter x1 -> x0, waiting for transfers between devices: 99.9 us -> none  [on_device(): lax.psum_scatter(term_all, ('inner', 'outer'), scatter_dimension=0, tiled...]
    dot_general x56 -> x0, matrix products: 65.1 us -> none  [the longest x16 22.6 us: scores(): jnp.einsum('tgud,pud->tgup', query_head_rows, key_heads, preferred_elemen...]
    ppermute x0 -> x22, starting transfers between devices: none -> 35.6 us  [send(): return lax.ppermute(x, AXES, pairs)]
    pallas_call x0 -> x8, Pallas kernels: none -> 18.6 us  [call(): pl.pallas_call(kernel, out_shape=outs, in_specs=[SMEM, SMEM] + [VMEM] * (...]
    ppermute x0 -> x22, waiting for transfers between devices: none -> 15.3 us  [send(): return lax.ppermute(x, AXES, pairs)]
    all_to_all x4 -> x2, starting transfers between devices: 17.6 us -> 7.77 us  [the longest x1 4.27 us: on_device(): lax.all_to_all(jnp.transpose(qd, (2, 0, 1, 3)), 'head', 0, 0, tiled=True)]
    dynamic_update_slice x16 -> x0, local copies, waits for them, and re-layouts: 8.34 us -> none  [add_back(): term_all = lax.dynamic_update_slice_in_dim(term_all, fresh_rows, start, 0)]
  transfers between devices with their start and end apart: 7 -> 24, of which waited for: 6 -> 10; matrix products, arithmetic and copies ran while one was open for 12% -> 5% of each run, Pallas kernels for 0% -> 15%
where the time goes in v1:
time: 92.7 us; the launch traced here: 91.7 us
  starting transfers between devices  43.4 us (47%)
  waiting for transfers between devices  22.2 us (24%)
  Pallas kernels  18.6 us (20%)
  local copies, waits for them, and re-layouts  4.23 us (5%)
  other arithmetic  2.42 us (3%)
    ppermute x22, starting transfers between devices, send(): return lax.ppermute(x, AXES, pairs)  35.6 us
    pallas_call x8, Pallas kernels, call(): pl.pallas_call(kernel, out_shape=outs, in_specs=[SMEM, SMEM] + [VMEM] * (...  18.6 us
    ppermute x22, waiting for transfers between devices, send(): return lax.ppermute(x, AXES, pairs)  15.3 us
    all_to_all x1, waiting for transfers between devices, on_device(): lax.all_to_all(jnp.transpose(qd, (2, 0, 1, 3)), 'head', 0, 0, tiled=True)  6.93 us
    all_to_all x1, starting transfers between devices, on_device(): lax.all_to_all(jnp.transpose(qd, (2, 0, 1, 3)), 'head', 0, 0, tiled=True)  4.27 us
    all_to_all x1, starting transfers between devices, on_device(): back = lax.all_to_all(back, 'head', 0, 0, tiled=True)  3.5 us
    unnamed x12, local copies, waits for them, and re-layouts  2.82 us
  transfers between devices with their start and end apart: 24, of which 10 were waited for; matrix products, arithmetic and copies ran while one was open for 5% of the time, Pallas kernels for 15%

profile of v1, /device:TPU:1, one launch (start us, length us, event | category | flops | bytes accessed | tf_op | source)
XLA Modules:
  0.0 91.7 jit_solution(8744900506901391205)
XLA Ops:
  1.4 4.4 %collective-permute-start.2 = (bf16[2,128,128]{2,1,0:T(8,128)(2,1)S(1)}, bf16[2,128,128]{2,1,0:T(8,128)(2,1)S(1)}, u32[]{:S(2)}, u32[]{:S(2)}) collective-permute-start(bf16[2,128,128]{2,1,0:T(8,128)(2,1)S(1)} %get-tuple-element.76), channel_id=1, source_target_pairs={{0,3},{1,2},{2,1},{3,0},{4,7},{5,6},{6,5},{7,4},{8,11},{9,10},{10,... | collective-permute-start | bytes 196616 | tf_op jit(solution)/shard_map/ppermute | solution.py:253
  7.8 3.4 %collective-permute-done = bf16[2,128,128]{2,1,0:T(8,128)(2,1)S(1)} collective-permute-done((bf16[2,128,128]{2,1,0:T(8,128)(2,1)S(1)}, bf16[2,128,128]{2,1,0:T(8,128)(2,1)S(1)}, u32[]{:S(2)}, u32[]{:S(2)}) %collective-permute-start) | collective-permute-done | bytes 65568 | tf_op jit(solution)/shard_map/ppermute | solution.py:253
  11.2 5.7 %collective-permute-start.3 = (bf16[4,2,128,128]{3,2,1,0:T(8,128)(2,1)S(1)}, bf16[4,2,128,128]{3,2,1,0:T(8,128)(2,1)S(1)}, u32[]{:S(2)}, u32[]{:S(2)}) collective-permute-start(bf16[4,2,128,128]{3,2,1,0:T(8,128)(2,1)S(1)} %pad_maximum_fusion.refs_3_.refs_4_), channel_id=1, source_target_pairs={{0,4},{1,29},{2,6},{3,31},{4,8},{5,1},{6,10},{7,3},{8,12},{9,5},{1... | collective-permute-start | bytes 786440 | tf_op jit(solution)/shard_map/ppermute | solution.py:253
  18.3 1.8 %collective-permute-done.3.refs_4_.refs_5_ = bf16[4,2,128,128]{3,2,1,0:T(8,128)(2,1)S(1)} collective-permute-done((bf16[4,2,128,128]{3,2,1,0:T(8,128)(2,1)S(1)}, bf16[4,2,128,128]{3,2,1,0:T(8,128)(2,1)S(1)}, u32[]{:S(2)}, u32[]{:S(2)}) %collective-permute-start.3) | collective-permute-done | bytes 262176 | tf_op jit(solution)/shard_map/ppermute | solution.py:253
  20.1 3.1 %collective-permute-start.4 = (bf16[4,2,128,128]{3,2,1,0:T(8,128)(2,1)S(1)}, bf16[4,2,128,128]{3,2,1,0:T(8,128)(2,1)S(1)}, u32[]{:S(2)}, u32[]{:S(2)}) collective-permute-start(bf16[4,2,128,128]{3,2,1,0:T(8,128)(2,1)S(1)} %collective-permute-done.3.refs_4_.refs_5_), channel_id=1, source_target_pairs={{0,4},{1,29},{2,6},{3,31},{4,8},{5,1},{6,10},{7,3},{8,12},{9,5},{1... | collective-permute-start | bytes 786440 | tf_op jit(solution)/shard_map/ppermute | solution.py:253
  24.1 4.3 %all-to-all-start = ((bf16[8,2,128,128]{3,2,1,0:T(8,128)(2,1)}), bf16[8,2,128,128]{3,2,1,0:T(8,128)(2,1)S(1)}, u32[]{:S(2)}, u32[]{:S(2)}) async-start(bf16[8,2,128,128]{3,2,1,0:T(8,128)(2,1)} %maximum_bitcast_fusion), calls=%async_computation | async-start | bytes 1048576 | tf_op jit(solution)/shard_map/all_to_all | solution.py:273
  28.5 2.1 %collective-permute-start.5 = (bf16[4,2,128,128]{3,2,1,0:T(8,128)(2,1)S(1)}, bf16[4,2,128,128]{3,2,1,0:T(8,128)(2,1)S(1)}, u32[]{:S(2)}, u32[]{:S(2)}) collective-permute-start(bf16[4,2,128,128]{3,2,1,0:T(8,128)(2,1)S(1)} %collective-permute-done.4.refs_4_.refs_5_), channel_id=1, source_target_pairs={{0,4},{1,29},{2,6},{3,31},{4,8},{5,1},{6,10},{7,3},{8,12},{9,5},{1... | collective-permute-start | bytes 786440 | tf_op jit(solution)/shard_map/ppermute | solution.py:253
  30.9 6.9 %all-to-all-done.refs_2_ = bf16[8,2,128,128]{3,2,1,0:T(8,128)(2,1)S(1)} async-done(((bf16[8,2,128,128]{3,2,1,0:T(8,128)(2,1)}), bf16[8,2,128,128]{3,2,1,0:T(8,128)(2,1)S(1)}, u32[]{:S(2)}, u32[]{:S(2)}) %all-to-all-start) | async-done | bytes 524320 | tf_op jit(solution)/shard_map/all_to_all | solution.py:273
  37.8 1.8 %shard_map.93 = (f32[2,2,8,512]{3,2,1,0:T(8,128)S(1)}, f32[2,128,512]{2,1,0:T(8,128)S(1)}) custom-call(s32[64]{0:T(128)S(1)} %copy-done, s32[5]{0:T(128)S(1)} %pad_add_fusion.refs_1_, bf16[8,2,128,128]{3,2,1,0:T(8,128)(2,1)S(1)} %all-to-all-done.refs_2_, bf16[4,2,128,128]{3,2,1,0:T(8,128)(2,1)S(1)} %pad_maximum_fusion.refs_3_.refs_4_, ...), custom_call_target="tpu_custom_call" | custom-call | flops 500000000 | bytes 2000000 | tf_op jit(solution)/shard_map/pallas_call | solution.py:204
  41.2 2.3 %shard_map.94 = (f32[2,2,8,512]{3,2,1,0:T(8,128)S(1)}, f32[2,128,512]{2,1,0:T(8,128)S(1)}) custom-call(s32[64]{0:T(128)S(1)} %copy-done, s32[5]{0:T(128)S(1)} %pad_add_fusion.refs_1_, bf16[8,2,128,128]{3,2,1,0:T(8,128)(2,1)S(1)} %all-to-all-done.refs_2_, bf16[4,2,128,128]{3,2,1,0:T(8,128)(2,1)S(1)} %collective-permute-done.9.refs_3_.refs_4_, ...), custom_call_target="tpu_custom_call" | custom-call | flops 500000000 | bytes 2000000 | tf_op jit(solution)/shard_map/pallas_call | solution.py:204
  43.6 1.8 %shard_map.95 = (f32[2,2,8,512]{3,2,1,0:T(8,128)S(1)}, f32[2,128,512]{2,1,0:T(8,128)S(1)}) custom-call(s32[64]{0:T(128)S(1)} %copy-done, s32[5]{0:T(128)S(1)} %pad_add_fusion.refs_1_, bf16[8,2,128,128]{3,2,1,0:T(8,128)(2,1)S(1)} %all-to-all-done.refs_2_, bf16[4,2,128,128]{3,2,1,0:T(8,128)(2,1)S(1)} %collective-permute-done.8.refs_3_.refs_4_, ...), custom_call_target="tpu_custom_call" | custom-call | flops 500000000 | bytes 2000000 | tf_op jit(solution)/shard_map/pallas_call | solution.py:204
  45.4 1.9 %collective-permute-start.10 = (bf16[2,2,128,128]{3,2,1,0:T(8,128)(2,1)S(1)}, bf16[2,2,128,128]{3,2,1,0:T(8,128)(2,1)S(1)}, u32[]{:S(2)}, u32[]{:S(2)}) collective-permute-start(bf16[2,2,128,128]{3,2,1,0:T(8,128)(2,1)S(1)} %collective-permute-done.7.refs_4_.refs_5_), channel_id=1, source_target_pairs={{0,1},{1,0},{2,3},{3,2},{4,5},{5,4},{6,7},{7,6},{8,9},{9,8},{10,11... | collective-permute-start | bytes 393224 | tf_op jit(solution)/shard_map/ppermute | solution.py:253
  48.3 2.5 %shard_map.96 = (f32[2,2,8,512]{3,2,1,0:T(8,128)S(1)}, bf16[8,128,128]{2,1,0:T(8,128)(2,1)S(1)}) custom-call(s32[64]{0:T(128)S(1)} %copy-done, s32[5]{0:T(128)S(1)} %pad_add_fusion.refs_1_, bf16[8,2,128,128]{3,2,1,0:T(8,128)(2,1)S(1)} %all-to-all-done.refs_2_, bf16[4,2,128,128]{3,2,1,0:T(8,128)(2,1)S(1)} %collective-permute-done.6.refs_3_.refs_4_, ...), custom_call_target="tpu_custom_call" | custom-call | flops 500000000 | bytes 2000000 | tf_op jit(solution)/shard_map/pallas_call | solution.py:204
  50.8 2.7 %shard_map.97 = (bf16[4,2,128,128]{3,2,1,0:T(8,128)(2,1)S(1)}, bf16[2,2,128,128]{3,2,1,0:T(8,128)(2,1)S(1)}, bf16[2,2,128,128]{3,2,1,0:T(8,128)(2,1)S(1)}, f32[2,128,512]{2,1,0:T(8,128)S(1)}) custom-call(s32[64]{0:T(128)S(1)} %copy-done, s32[5]{0:T(128)S(1)} %pad_add_fusion.refs_1_, bf16[8,2,128,128]{3,2,1,0:T(8,128)(2,1)S(1)} %all-to-all-done.refs_2_, ...), custom_call_target="tpu_custom_call" | custom-call | flops 1000000000 | bytes 2000000 | tf_op jit(solution)/shard_map/pallas_call | solution.py:204
  55.1 2.0 %shard_map.98 = (bf16[4,2,128,128]{3,2,1,0:T(8,128)(2,1)S(1)}, bf16[4,2,128,128]{3,2,1,0:T(8,128)(2,1)S(1)}, f32[2,128,512]{2,1,0:T(8,128)S(1)}) custom-call(s32[64]{0:T(128)S(1)} %copy-done, s32[5]{0:T(128)S(1)} %pad_add_fusion.refs_1_, bf16[8,2,128,128]{3,2,1,0:T(8,128)(2,1)S(1)} %all-to-all-done.refs_2_, f32[2,2,8,512]{3,2,1,0:T(8,128)S(1)} %get-tuple-element.43.refs_3_, ...), custom_call_target="tpu_custom_call" | custom-call | flops 1000000000 | bytes 2000000 | tf_op jit(solution)/shard_map/pallas_call | solution.py:204
  57.1 3.4 %collective-permute-start.12 = (bf16[4,2,128,128]{3,2,1,0:T(8,128)(2,1)S(1)}, bf16[4,2,128,128]{3,2,1,0:T(8,128)(2,1)S(1)}, u32[]{:S(2)}, u32[]{:S(2)}) collective-permute-start(bf16[4,2,128,128]{3,2,1,0:T(8,128)(2,1)S(1)} %get-tuple-element.53), channel_id=1, source_target_pairs={{0,1},{1,0},{2,3},{3,2},{4,5},{5,4},{6,7},{7,6},{8,9},{9,8},{10,11... | collective-permute-start | bytes 786440 | tf_op jit(solution)/shard_map/ppermute | solution.py:253
  60.7 2.5 %shard_map.99 = (bf16[4,2,128,128]{3,2,1,0:T(8,128)(2,1)S(1)}, bf16[4,2,128,128]{3,2,1,0:T(8,128)(2,1)S(1)}, f32[2,128,512]{2,1,0:T(8,128)S(1)}) custom-call(s32[64]{0:T(128)S(1)} %copy-done, s32[5]{0:T(128)S(1)} %pad_add_fusion.refs_1_, bf16[8,2,128,128]{3,2,1,0:T(8,128)(2,1)S(1)} %all-to-all-done.refs_2_, f32[2,2,8,512]{3,2,1,0:T(8,128)S(1)} %get-tuple-element.43.refs_3_, ...), custom_call_target="tpu_custom_call" | custom-call | flops 1000000000 | bytes 2000000 | tf_op jit(solution)/shard_map/pallas_call | solution.py:204
  63.3 3.6 %collective-permute-start.11 = (bf16[4,2,128,128]{3,2,1,0:T(8,128)(2,1)S(1)}, bf16[4,2,128,128]{3,2,1,0:T(8,128)(2,1)S(1)}, u32[]{:S(2)}, u32[]{:S(2)}) collective-permute-start(bf16[4,2,128,128]{3,2,1,0:T(8,128)(2,1)S(1)} %get-tuple-element.51), channel_id=1, source_target_pairs={{0,1},{1,0},{2,3},{3,2},{4,5},{5,4},{6,7},{7,6},{8,9},{9,8},{10,11... | collective-permute-start | bytes 786440 | tf_op jit(solution)/shard_map/ppermute | solution.py:253
  67.4 2.9 %shard_map.100 = (bf16[4,2,128,128]{3,2,1,0:T(8,128)(2,1)S(1)}, bf16[4,2,128,128]{3,2,1,0:T(8,128)(2,1)S(1)}, bf16[8,2,128,128]{3,2,1,0:T(8,128)(2,1)}) custom-call(s32[64]{0:T(128)S(1)} %copy-done, s32[5]{0:T(128)S(1)} %pad_add_fusion.refs_1_, bf16[8,2,128,128]{3,2,1,0:T(8,128)(2,1)S(1)} %all-to-all-done.refs_2_, ...), custom_call_target="tpu_custom_call" | custom-call | flops 1000000000 | bytes 2000000 | tf_op jit(solution)/shard_map/pallas_call | solution.py:204
  70.2 3.6 %collective-permute-done.17 = bf16[4,2,128,128]{3,2,1,0:T(8,128)(2,1)S(1)} collective-permute-done((bf16[4,2,128,128]{3,2,1,0:T(8,128)(2,1)S(1)}, bf16[4,2,128,128]{3,2,1,0:T(8,128)(2,1)S(1)}, u32[]{:S(2)}, u32[]{:S(2)}) %collective-permute-start.17) | collective-permute-done | bytes 262176 | tf_op jit(solution)/shard_map/ppermute | solution.py:253
  74.0 3.5 %all-to-all-start.1 = ((bf16[8,2,128,128]{3,2,1,0:T(8,128)(2,1)}), bf16[8,2,128,128]{3,2,1,0:T(8,128)(2,1)S(1)}, u32[]{:S(2)}, u32[]{:S(2)}) async-start(bf16[8,2,128,128]{3,2,1,0:T(8,128)(2,1)} %get-tuple-element.48), calls=%async_computation.1 | async-start | bytes 1048576 | tf_op jit(solution)/shard_map/all_to_all | solution.py:306
  77.5 2.9 %collective-permute-done.18 = bf16[4,2,128,128]{3,2,1,0:T(8,128)(2,1)S(1)} collective-permute-done((bf16[4,2,128,128]{3,2,1,0:T(8,128)(2,1)S(1)}, bf16[4,2,128,128]{3,2,1,0:T(8,128)(2,1)S(1)}, u32[]{:S(2)}, u32[]{:S(2)}) %collective-permute-start.18) | collective-permute-done | bytes 262176 | tf_op jit(solution)/shard_map/ppermute | solution.py:253
  80.6 3.9 %collective-permute-start.20 = (bf16[2,128,128]{2,1,0:T(8,128)(2,1)S(1)}, bf16[2,128,128]{2,1,0:T(8,128)(2,1)S(1)}, u32[]{:S(2)}, u32[]{:S(2)}) collective-permute-start(bf16[2,128,128]{2,1,0:T(8,128)(2,1)S(1)} %get-tuple-element.72), channel_id=1, source_target_pairs={{0,1},{1,0},{2,3},{3,2},{4,5},{5,4},{6,7},{7,6},{8,9},{9,8},{10,11... | collective-permute-start | bytes 196616 | tf_op jit(solution)/shard_map/ppermute | solution.py:253
  84.5 3.0 %collective-permute-start.21 = (bf16[2,128,128]{2,1,0:T(8,128)(2,1)S(1)}, bf16[2,128,128]{2,1,0:T(8,128)(2,1)S(1)}, u32[]{:S(2)}, u32[]{:S(2)}) collective-permute-start(bf16[2,128,128]{2,1,0:T(8,128)(2,1)S(1)} %get-tuple-element.71), channel_id=1, source_target_pairs={{0,3},{1,2},{2,1},{3,0},{4,7},{5,6},{6,5},{7,4},{8,11},{9,10},{10,... | collective-permute-start | bytes 196616 | tf_op jit(solution)/shard_map/ppermute | solution.py:253
  (64 shorter events, 14.7 us)
Async XLA Ops:
  1.4 6.3 %collective-permute-start.2 = (bf16[2,128,128]{2,1,0:T(8,128)(2,1)S(1)}, bf16[2,128,128]{2,1,0:T(8,128)(2,1)S(1)}, u32[]{:S(2)}, u32[]{:S(2)}) collective-permute-start(bf16[2,128,128]{2,1,0:T(8,128)(2,1)S(1)} %get-tuple-element.76), channel_id=1, source_target_pairs={{0,3},{1,2},{2,1},{3,0},{4,7},{5,6},{6,5},{7,4},{8,11},{9,10},{10,... | collective-permute-start | bytes 196616 | tf_op jit(solution)/shard_map/ppermute | solution.py:253
  5.8 5.3 %collective-permute-start = (bf16[2,128,128]{2,1,0:T(8,128)(2,1)S(1)}, bf16[2,128,128]{2,1,0:T(8,128)(2,1)S(1)}, u32[]{:S(2)}, u32[]{:S(2)}) collective-permute-start(bf16[2,128,128]{2,1,0:T(8,128)(2,1)S(1)} %get-tuple-element.76), channel_id=1, source_target_pairs={{0,2},{1,3},{2,0},{3,1},{4,6},{5,7},{6,4},{7,5},{8,10},{9,11},{10,... | collective-permute-start | bytes 196616 | tf_op jit(solution)/shard_map/ppermute | solution.py:253
  7.6 3.5 %collective-permute-start.1 = (bf16[2,128,128]{2,1,0:T(8,128)(2,1)S(1)}, bf16[2,128,128]{2,1,0:T(8,128)(2,1)S(1)}, u32[]{:S(2)}, u32[]{:S(2)}) collective-permute-start(bf16[2,128,128]{2,1,0:T(8,128)(2,1)S(1)} %get-tuple-element.76), channel_id=1, source_target_pairs={{0,1},{1,0},{2,3},{3,2},{4,5},{5,4},{6,7},{7,6},{8,9},{9,8},{10,11... | collective-permute-start | bytes 196616 | tf_op jit(solution)/shard_map/ppermute | solution.py:253
  11.2 9.0 %collective-permute-start.3 = (bf16[4,2,128,128]{3,2,1,0:T(8,128)(2,1)S(1)}, bf16[4,2,128,128]{3,2,1,0:T(8,128)(2,1)S(1)}, u32[]{:S(2)}, u32[]{:S(2)}) collective-permute-start(bf16[4,2,128,128]{3,2,1,0:T(8,128)(2,1)S(1)} %pad_maximum_fusion.refs_3_.refs_4_), channel_id=1, source_target_pairs={{0,4},{1,29},{2,6},{3,31},{4,8},{5,1},{6,10},{7,3},{8,12},{9,5},{1... | collective-permute-start | bytes 786440 | tf_op jit(solution)/shard_map/ppermute | solution.py:253
  20.1 8.3 %collective-permute-start.4 = (bf16[4,2,128,128]{3,2,1,0:T(8,128)(2,1)S(1)}, bf16[4,2,128,128]{3,2,1,0:T(8,128)(2,1)S(1)}, u32[]{:S(2)}, u32[]{:S(2)}) collective-permute-start(bf16[4,2,128,128]{3,2,1,0:T(8,128)(2,1)S(1)} %collective-permute-done.3.refs_4_.refs_5_), channel_id=1, source_target_pairs={{0,4},{1,29},{2,6},{3,31},{4,8},{5,1},{6,10},{7,3},{8,12},{9,5},{1... | collective-permute-start | bytes 786440 | tf_op jit(solution)/shard_map/ppermute | solution.py:253
  24.1 13.7 %all-to-all-start = ((bf16[8,2,128,128]{3,2,1,0:T(8,128)(2,1)}), bf16[8,2,128,128]{3,2,1,0:T(8,128)(2,1)S(1)}, u32[]{:S(2)}, u32[]{:S(2)}) async-start(bf16[8,2,128,128]{3,2,1,0:T(8,128)(2,1)} %maximum_bitcast_fusion), calls=%async_computation | async-start | bytes 1048576 | tf_op jit(solution)/shard_map/all_to_all | solution.py:273
  28.4 12.8 %collective-permute-start.9 = (bf16[4,2,128,128]{3,2,1,0:T(8,128)(2,1)S(1)}, bf16[4,2,128,128]{3,2,1,0:T(8,128)(2,1)S(1)}, u32[]{:S(2)}, u32[]{:S(2)}) collective-permute-start(bf16[4,2,128,128]{3,2,1,0:T(8,128)(2,1)S(1)} %collective-permute-done.3.refs_4_.refs_5_), channel_id=1, source_target_pairs={{0,1},{1,0},{2,3},{3,2},{4,5},{5,4},{6,7},{7,6},{8,9},{9,8},{10,11... | collective-permute-start | bytes 786440 | tf_op jit(solution)/shard_map/ppermute | solution.py:253
  28.5 11.2 %collective-permute-start.5 = (bf16[4,2,128,128]{3,2,1,0:T(8,128)(2,1)S(1)}, bf16[4,2,128,128]{3,2,1,0:T(8,128)(2,1)S(1)}, u32[]{:S(2)}, u32[]{:S(2)}) collective-permute-start(bf16[4,2,128,128]{3,2,1,0:T(8,128)(2,1)S(1)} %collective-permute-done.4.refs_4_.refs_5_), channel_id=1, source_target_pairs={{0,4},{1,29},{2,6},{3,31},{4,8},{5,1},{6,10},{7,3},{8,12},{9,5},{1... | collective-permute-start | bytes 786440 | tf_op jit(solution)/shard_map/ppermute | solution.py:253
  30.6 13.0 %collective-permute-start.8 = (bf16[4,2,128,128]{3,2,1,0:T(8,128)(2,1)S(1)}, bf16[4,2,128,128]{3,2,1,0:T(8,128)(2,1)S(1)}, u32[]{:S(2)}, u32[]{:S(2)}) collective-permute-start(bf16[4,2,128,128]{3,2,1,0:T(8,128)(2,1)S(1)} %collective-permute-done.4.refs_4_.refs_5_), channel_id=1, source_target_pairs={{0,1},{1,0},{2,3},{3,2},{4,5},{5,4},{6,7},{7,6},{8,9},{9,8},{10,11... | collective-permute-start | bytes 786440 | tf_op jit(solution)/shard_map/ppermute | solution.py:253
  39.7 5.7 %collective-permute-start.7 = (bf16[2,2,128,128]{3,2,1,0:T(8,128)(2,1)S(1)}, bf16[2,2,128,128]{3,2,1,0:T(8,128)(2,1)S(1)}, u32[]{:S(2)}, u32[]{:S(2)}) collective-permute-start(bf16[2,2,128,128]{3,2,1,0:T(8,128)(2,1)S(1)} %slice.29), channel_id=1, source_target_pairs={{0,4},{1,29},{2,6},{3,31},{4,8},{5,1},{6,10},{7,3},{8,12},{9,5},{1... | collective-permute-start | bytes 393224 | tf_op jit(solution)/shard_map/ppermute | solution.py:253
  39.8 8.5 %collective-permute-start.6 = (bf16[4,2,128,128]{3,2,1,0:T(8,128)(2,1)S(1)}, bf16[4,2,128,128]{3,2,1,0:T(8,128)(2,1)S(1)}, u32[]{:S(2)}, u32[]{:S(2)}) collective-permute-start(bf16[4,2,128,128]{3,2,1,0:T(8,128)(2,1)S(1)} %collective-permute-done.5.refs_4_.refs_5_), channel_id=1, source_target_pairs={{0,1},{1,0},{2,3},{3,2},{4,5},{5,4},{6,7},{7,6},{8,9},{9,8},{10,11... | collective-permute-start | bytes 786440 | tf_op jit(solution)/shard_map/ppermute | solution.py:253
  45.4 2.9 %collective-permute-start.10 = (bf16[2,2,128,128]{3,2,1,0:T(8,128)(2,1)S(1)}, bf16[2,2,128,128]{3,2,1,0:T(8,128)(2,1)S(1)}, u32[]{:S(2)}, u32[]{:S(2)}) collective-permute-start(bf16[2,2,128,128]{3,2,1,0:T(8,128)(2,1)S(1)} %collective-permute-done.7.refs_4_.refs_5_), channel_id=1, source_target_pairs={{0,1},{1,0},{2,3},{3,2},{4,5},{5,4},{6,7},{7,6},{8,9},{9,8},{10,11... | collective-permute-start | bytes 393224 | tf_op jit(solution)/shard_map/ppermute | solution.py:253
  53.6 1.4 %collective-permute-start.14 = (bf16[2,2,128,128]{3,2,1,0:T(8,128)(2,1)S(1)}, bf16[2,2,128,128]{3,2,1,0:T(8,128)(2,1)S(1)}, u32[]{:S(2)}, u32[]{:S(2)}) collective-permute-start(bf16[2,2,128,128]{3,2,1,0:T(8,128)(2,1)S(1)} %get-tuple-element.57), channel_id=1, source_target_pairs={{0,1},{1,0},{2,3},{3,2},{4,5},{5,4},{6,7},{7,6},{8,9},{9,8},{10,11... | collective-permute-start | bytes 393224 | tf_op jit(solution)/shard_map/ppermute | solution.py:253
  54.0 6.5 %collective-permute-start.13 = (bf16[4,2,128,128]{3,2,1,0:T(8,128)(2,1)S(1)}, bf16[4,2,128,128]{3,2,1,0:T(8,128)(2,1)S(1)}, u32[]{:S(2)}, u32[]{:S(2)}) collective-permute-start(bf16[4,2,128,128]{3,2,1,0:T(8,128)(2,1)S(1)} %get-tuple-element.55), channel_id=1, source_target_pairs={{0,1},{1,0},{2,3},{3,2},{4,5},{5,4},{6,7},{7,6},{8,9},{9,8},{10,11... | collective-permute-start | bytes 786440 | tf_op jit(solution)/shard_map/ppermute | solution.py:253
  55.0 5.5 %collective-permute-start.15 = (bf16[2,2,128,128]{3,2,1,0:T(8,128)(2,1)S(1)}, bf16[2,2,128,128]{3,2,1,0:T(8,128)(2,1)S(1)}, u32[]{:S(2)}, u32[]{:S(2)}) collective-permute-start(bf16[2,2,128,128]{3,2,1,0:T(8,128)(2,1)S(1)} %add_convert_fusion.3), channel_id=1, source_target_pairs={{0,28},{1,5},{2,30},{3,7},{4,0},{5,9},{6,2},{7,11},{8,4},{9,13},{1... | collective-permute-start | bytes 393224 | tf_op jit(solution)/shard_map/ppermute | solution.py:253
  57.1 9.8 %collective-permute-start.12 = (bf16[4,2,128,128]{3,2,1,0:T(8,128)(2,1)S(1)}, bf16[4,2,128,128]{3,2,1,0:T(8,128)(2,1)S(1)}, u32[]{:S(2)}, u32[]{:S(2)}) collective-permute-start(bf16[4,2,128,128]{3,2,1,0:T(8,128)(2,1)S(1)} %get-tuple-element.53), channel_id=1, source_target_pairs={{0,1},{1,0},{2,3},{3,2},{4,5},{5,4},{6,7},{7,6},{8,9},{9,8},{10,11... | collective-permute-start | bytes 786440 | tf_op jit(solution)/shard_map/ppermute | solution.py:253
  60.6 6.5 %collective-permute-start.16 = (bf16[4,2,128,128]{3,2,1,0:T(8,128)(2,1)S(1)}, bf16[4,2,128,128]{3,2,1,0:T(8,128)(2,1)S(1)}, u32[]{:S(2)}, u32[]{:S(2)}) collective-permute-start(bf16[4,2,128,128]{3,2,1,0:T(8,128)(2,1)S(1)} %add_convert_fusion.2), channel_id=1, source_target_pairs={{0,28},{1,5},{2,30},{3,7},{4,0},{5,9},{6,2},{7,11},{8,4},{9,13},{1... | collective-permute-start | bytes 786440 | tf_op jit(solution)/shard_map/ppermute | solution.py:253
  63.3 6.9 %collective-permute-start.11 = (bf16[4,2,128,128]{3,2,1,0:T(8,128)(2,1)S(1)}, bf16[4,2,128,128]{3,2,1,0:T(8,128)(2,1)S(1)}, u32[]{:S(2)}, u32[]{:S(2)}) collective-permute-start(bf16[4,2,128,128]{3,2,1,0:T(8,128)(2,1)S(1)} %get-tuple-element.51), channel_id=1, source_target_pairs={{0,1},{1,0},{2,3},{3,2},{4,5},{5,4},{6,7},{7,6},{8,9},{9,8},{10,11... | collective-permute-start | bytes 786440 | tf_op jit(solution)/shard_map/ppermute | solution.py:253
  67.3 6.5 %collective-permute-start.17 = (bf16[4,2,128,128]{3,2,1,0:T(8,128)(2,1)S(1)}, bf16[4,2,128,128]{3,2,1,0:T(8,128)(2,1)S(1)}, u32[]{:S(2)}, u32[]{:S(2)}) collective-permute-start(bf16[4,2,128,128]{3,2,1,0:T(8,128)(2,1)S(1)} %add_convert_fusion.1), channel_id=1, source_target_pairs={{0,28},{1,5},{2,30},{3,7},{4,0},{5,9},{6,2},{7,11},{8,4},{9,13},{1... | collective-permute-start | bytes 786440 | tf_op jit(solution)/shard_map/ppermute | solution.py:253
  73.9 6.5 %collective-permute-start.18 = (bf16[4,2,128,128]{3,2,1,0:T(8,128)(2,1)S(1)}, bf16[4,2,128,128]{3,2,1,0:T(8,128)(2,1)S(1)}, u32[]{:S(2)}, u32[]{:S(2)}) collective-permute-start(bf16[4,2,128,128]{3,2,1,0:T(8,128)(2,1)S(1)} %add_convert_fusion), channel_id=1, source_target_pairs={{0,28},{1,5},{2,30},{3,7},{4,0},{5,9},{6,2},{7,11},{8,4},{9,13},{1... | collective-permute-start | bytes 786440 | tf_op jit(solution)/shard_map/ppermute | solution.py:253
  74.0 13.6 %all-to-all-start.1 = ((bf16[8,2,128,128]{3,2,1,0:T(8,128)(2,1)}), bf16[8,2,128,128]{3,2,1,0:T(8,128)(2,1)S(1)}, u32[]{:S(2)}, u32[]{:S(2)}) async-start(bf16[8,2,128,128]{3,2,1,0:T(8,128)(2,1)} %get-tuple-element.48), calls=%async_computation.1 | async-start | bytes 1048576 | tf_op jit(solution)/shard_map/all_to_all | solution.py:306
  80.5 9.2 %collective-permute-start.19 = (bf16[2,128,128]{2,1,0:T(8,128)(2,1)S(1)}, bf16[2,128,128]{2,1,0:T(8,128)(2,1)S(1)}, u32[]{:S(2)}, u32[]{:S(2)}) collective-permute-start(bf16[2,128,128]{2,1,0:T(8,128)(2,1)S(1)} %get-tuple-element.70), channel_id=1, source_target_pairs={{0,2},{1,3},{2,0},{3,1},{4,6},{5,7},{6,4},{7,5},{8,10},{9,11},{10,... | collective-permute-start | bytes 196616 | tf_op jit(solution)/shard_map/ppermute | solution.py:253
  80.6 9.1 %collective-permute-start.20 = (bf16[2,128,128]{2,1,0:T(8,128)(2,1)S(1)}, bf16[2,128,128]{2,1,0:T(8,128)(2,1)S(1)}, u32[]{:S(2)}, u32[]{:S(2)}) collective-permute-start(bf16[2,128,128]{2,1,0:T(8,128)(2,1)S(1)} %get-tuple-element.72), channel_id=1, source_target_pairs={{0,1},{1,0},{2,3},{3,2},{4,5},{5,4},{6,7},{7,6},{8,9},{9,8},{10,11... | collective-permute-start | bytes 196616 | tf_op jit(solution)/shard_map/ppermute | solution.py:253
  84.5 6.5 %collective-permute-start.21 = (bf16[2,128,128]{2,1,0:T(8,128)(2,1)S(1)}, bf16[2,128,128]{2,1,0:T(8,128)(2,1)S(1)}, u32[]{:S(2)}, u32[]{:S(2)}) collective-permute-start(bf16[2,128,128]{2,1,0:T(8,128)(2,1)S(1)} %get-tuple-element.71), channel_id=1, source_target_pairs={{0,3},{1,2},{2,1},{3,0},{4,7},{5,6},{6,5},{7,4},{8,11},{9,10},{10,... | collective-permute-start | bytes 196616 | tf_op jit(solution)/shard_map/ppermute | solution.py:253
  (4 other events, 20.2 us)

commit v2 on v1

--- a/solution.py
+++ b/solution.py
@@ -28,17 +28,16 @@
 
 
 def blocks_of(kinds, refs, meta):
-    z, outer = meta[0], meta[1]
-    core = lax.rem(outer, 2)
+    z, y, core = meta[0], meta[1] // 2, lax.rem(meta[1], 2)
     for (side, steps), ref in zip(kinds, refs, strict=True):
         sign = (1 - 2 * core) * (1 if side == "near" else -1)
         chunk = lax.rem(z - sign * steps + 8, 8)
-        base = outer if side == "near" else outer + 1 - 2 * core
-        twin = base + 1 - 2 * lax.rem(base, 2)
-        shards = [base, lax.rem(base + 2, 4), twin, lax.rem(twin + 2, 4)]
+        c = core if side == "near" else 1 - core
+        first = lax.rem(y + c, 2) if steps else y
         for i in range(ref.shape[0]):
+            shard = 2 * (first if i < 2 else 1 - first) + (c if i % 2 == 0 else 1 - c)
             for b in range(2):
-                yield ref, i, b * BLOCK, chunk * 8 + shards[i] * 2 + b
+                yield ref, i, b * BLOCK, chunk * 8 + shard * 2 + b
 
 
 def limits(perm, meta, qb):
@@ -244,9 +243,10 @@
 AXES = ("inner", "outer")
 CORE = outer_perm(lambda z, y, c: (z, y, 1 - c))
 TWIN = outer_perm(lambda z, y, c: (z, 1 - y, c))
-CROSS = outer_perm(lambda z, y, c: (z, 1 - y, 1 - c))
 ONWARD = outer_perm(lambda z, y, c: (z + 1 - 2 * c, y, c))
 HOMEWARD = outer_perm(lambda z, y, c: (z - 1 + 2 * c, y, c))
+FIRST_ON = [outer_perm(lambda z, y, c, n=n: (z + 1 - 2 * c, (y + c + n) % 2, c)) for n in range(2)]
+LAST_HOME = [outer_perm(lambda z, y, c, n=n: (z - 1 + 2 * c, (y + c + n) % 2, c)) for n in range(2)]
 
 
 def send(x, pairs):
@@ -268,7 +268,9 @@
 def on_device(queries, keys, values, output_gradient, block_perm, segment_ids):
     rows = queries.shape[0]
     kv = jnp.stack([keys, values])
-    own = jnp.stack([kv, *(send(kv, pairs) for pairs in (TWIN, CORE, CROSS))])
+    pair = jnp.stack([kv, send(kv, CORE)])
+    near1 = jnp.concatenate([send(pair, pairs) for pairs in FIRST_ON])
+    own = jnp.concatenate([pair, send(pair, TWIN)])
     qd = jnp.stack([queries.reshape(rows, GROUP, HEAD), output_gradient.reshape(rows, GROUP, HEAD)])
     qd = lax.all_to_all(jnp.transpose(qd, (2, 0, 1, 3)), "head", 0, 0, tiled=True)
     starts = jnp.sum(segment_ids[None, :] < jnp.arange(1, 4, dtype=jnp.int32)[:, None], axis=1)
@@ -276,42 +278,38 @@
     meta = jnp.concatenate([place.astype(jnp.int32), starts.astype(jnp.int32)])
 
     run = functools.partial(forward, block_perm, meta, qd)
-    near1 = send(own, ONWARD)
-    calls = [((("near", 0), ("near", 1)), (own, near1))]
     near2 = send(near1, ONWARD)
-    far1 = send(near1, CORE)
-    state = run(*calls[0], None, False)
-    calls.append(((("far", 1), ("near", 2)), (far1, near2)))
     near3 = send(near2, ONWARD)
-    far2 = send(near2, CORE)
-    near3, *state = after(near3, *state)
-    state = run(*calls[1], state, False)
-    calls.append(((("far", 2), ("near", 3)), (far2, near3)))
-    near4 = send(near3[:2], ONWARD)
-    far3 = send(near3, CORE)
-    state = run(*calls[2], state, False)
+    state = run((("near", 1), ("near", 2)), (near1, near2), None, False)
+    near3, near1, near2, *state = after(near3, near1, near2, *state)
+    near4 = send(near3, ONWARD)
+    far1, far2, far3 = (send(x, CORE) for x in (near1, near2, near3))
+    state = run((("near", 3), ("near", 0)), (near3, own), state, False)
+    state = run((("far", 1), ("far", 2)), (far1, far2), state, False)
     near4, *state = after(near4, *state)
-    far4 = send(near4, CORE)
-    calls.append(((("far", 3), ("near", 4), ("far", 4)), (far3, near4, far4)))
-    stat, out = run(*calls[3], state, True)
+    stat, out = run((("far", 3), ("near", 4)), (far3, near4), state, True)
 
     run = functools.partial(backward, block_perm, meta, qd, stat)
-    far3, near4, far4, dqt = run(*calls[3], None, None)
-    far2, near3, dqt = run(*calls[2], dqt, None)
-    moving = send(add(near4, send(far4, CORE)), HOMEWARD)
-    far1, near2, dqt = run(*calls[1], dqt, None)
-    moving = jnp.concatenate([moving, jnp.zeros_like(moving)])
-    moving = send(add(near3, send(far3, CORE), moving), HOMEWARD)
-    own_grad, near1, back = run(*calls[0], dqt, out)
+    far3, near4, dqt = run((("far", 3), ("near", 4)), (far3, near4), None, None)
+    moving = send(near4, HOMEWARD)
+    far3 = send(far3, CORE)
+    near3, far2, dqt = run((("near", 3), ("far", 2)), (near3, far2), dqt, None)
+    near2, far1, dqt = run((("near", 2), ("far", 1)), (near2, far1), dqt, None)
+    moving, far2, dqt = after(moving, far2, dqt)
+    moving = send(add(near3, far3, moving), HOMEWARD)
+    far2 = send(far2, CORE)
+    near1, own, back = run((("near", 1), ("near", 0)), (near1, own), dqt, out)
+    moving, far1, own, back = after(moving, far1, own, back)
+    moving = send(add(near2, far2, moving), HOMEWARD)
+    far1 = send(far1, CORE)
+    own_twin = send(own[2:], TWIN)
     back = lax.all_to_all(back, "head", 0, 0, tiled=True)
-    moving = send(add(near2, send(far2, CORE), moving), HOMEWARD)
-    moving = send(add(near1, send(far1, CORE), moving), HOMEWARD)
-    total = total32(own_grad, moving)
-    sent = total.astype(BF16)
-    total = total[0] + total32(*(send(sent[i], pairs) for i, pairs in ((1, TWIN), (2, CORE), (3, CROSS))))
-    total = total.astype(BF16)
+    moving = add(near1, far1, moving)
+    pair = total32(own[:2], own_twin, *(send(moving[2 * n : 2 * n + 2], LAST_HOME[n]) for n in range(2)))
     back = jnp.transpose(back, (1, 2, 0, 3)).reshape(2, rows, GROUP * HEAD)
-    return back[0], back[1], total[0], total[1]
+    pair, attended, query_grad = after(pair, back[0], back[1])
+    total = add(pair[0], send(pair[1].astype(BF16), CORE))
+    return attended, query_grad, total[0], total[1]
 
 
 def solution(mesh):

time: 92.7 us -> 85.5 us (0.922)
  waiting for transfers between devices: 22.2 us -> 17.7 us
  starting transfers between devices: 43.4 us -> 41.3 us
    ppermute x22 -> x20, waiting for transfers between devices: 15.3 us -> 12.5 us  [send(): return lax.ppermute(x, AXES, pairs)]
    ppermute x22 -> x20, starting transfers between devices: 35.6 us -> 33.2 us  [send(): return lax.ppermute(x, AXES, pairs)]
    all_to_all x1, waiting for transfers between devices: 6.93 us -> 5.28 us  [on_device(): lax.all_to_all(jnp.transpose(qd, (2, 0, 1, 3)), 'head', 0, 0, tiled=True)]
    unnamed x12 -> x13, local copies, waits for them, and re-layouts: 2.82 us -> 2.82 us
  transfers between devices with their start and end apart: 24 -> 22, of which waited for: 10 -> 6; matrix products, arithmetic and copies ran while one was open for 5% -> 5% of each run, Pallas kernels for 15% -> 16%
where the time goes in v2:
time: 85.5 us; the launch traced here: 84.8 us
  starting transfers between devices  41.3 us (48%)
  Pallas kernels  18.1 us (21%)
  waiting for transfers between devices  17.7 us (21%)
  local copies, waits for them, and re-layouts  4.27 us (5%)
  other arithmetic  2.41 us (3%)
  between operations  0.97 us (1%)
    ppermute x20, starting transfers between devices, send(): return lax.ppermute(x, AXES, pairs)  33.2 us
    pallas_call x8, Pallas kernels, call(): pl.pallas_call(kernel, out_shape=outs, in_specs=[SMEM, SMEM] + [VMEM] * (...  18.1 us
    ppermute x20, waiting for transfers between devices, send(): return lax.ppermute(x, AXES, pairs)  12.5 us
    all_to_all x1, waiting for transfers between devices, on_device(): lax.all_to_all(jnp.transpose(qd, (2, 0, 1, 3)), 'head', 0, 0, tiled=True)  5.28 us
    all_to_all x1, starting transfers between devices, on_device(): lax.all_to_all(jnp.transpose(qd, (2, 0, 1, 3)), 'head', 0, 0, tiled=True)  4.59 us
    all_to_all x1, starting transfers between devices, on_device(): back = lax.all_to_all(back, 'head', 0, 0, tiled=True)  3.5 us
    unnamed x13, local copies, waits for them, and re-layouts  2.82 us
  transfers between devices with their start and end apart: 22, of which 6 were waited for; matrix products, arithmetic and copies ran while one was open for 5% of the time, Pallas kernels for 16%

profile of v2, /device:TPU:1, one launch (start us, length us, event | category | flops | bytes accessed | tf_op | source)
XLA Modules:
  0.0 84.8 jit_solution(4335389258404904062)
XLA Ops:
  1.5 3.3 %collective-permute-start = (bf16[2,128,128]{2,1,0:T(8,128)(2,1)S(1)}, bf16[2,128,128]{2,1,0:T(8,128)(2,1)S(1)}, u32[]{:S(2)}, u32[]{:S(2)}) collective-permute-start(bf16[2,128,128]{2,1,0:T(8,128)(2,1)S(1)} %get-tuple-element.95), channel_id=1, source_target_pairs={{0,1},{1,0},{2,3},{3,2},{4,5},{5,4},{6,7},{7,6},{8,9},{9,8},{10,11... | collective-permute-start | bytes 196616 | tf_op jit(solution)/shard_map/ppermute | solution.py:253
  5.7 6.5 %collective-permute-start.1 = (bf16[2,2,128,128]{3,2,1,0:T(8,128)(2,1)S(1)}, bf16[2,2,128,128]{3,2,1,0:T(8,128)(2,1)S(1)}, u32[]{:S(2)}, u32[]{:S(2)}) collective-permute-start(bf16[2,2,128,128]{3,2,1,0:T(8,128)(2,1)S(1)} %pad_maximum_fusion.1), channel_id=1, source_target_pairs={{0,4},{1,31},{2,6},{3,29},{4,8},{5,3},{6,10},{7,1},{8,12},{9,7},{1... | collective-permute-start | bytes 393224 | tf_op jit(solution)/shard_map/ppermute | solution.py:253
  14.5 1.9 %collective-permute-done.2 = bf16[2,2,128,128]{3,2,1,0:T(8,128)(2,1)S(1)} collective-permute-done((bf16[2,2,128,128]{3,2,1,0:T(8,128)(2,1)S(1)}, bf16[2,2,128,128]{3,2,1,0:T(8,128)(2,1)S(1)}, u32[]{:S(2)}, u32[]{:S(2)}) %collective-permute-start.2) | collective-permute-done | bytes 131104 | tf_op jit(solution)/shard_map/ppermute | solution.py:253
  16.4 2.4 %collective-permute-start.3 = (bf16[4,2,128,128]{3,2,1,0:T(8,128)(2,1)S(1)}, bf16[4,2,128,128]{3,2,1,0:T(8,128)(2,1)S(1)}, u32[]{:S(2)}, u32[]{:S(2)}) collective-permute-start(bf16[4,2,128,128]{3,2,1,0:T(8,128)(2,1)S(1)} %constant_dynamic-update-slice_fusion.refs_3_.refs_4_), channel_id=1, source_target_pairs={{0,4},{1,29},{2,6},{3,31},{4,8},{5,1},{6,10},{7,3},{8,12},{9,5},{1... | collective-permute-start | bytes 786440 | tf_op jit(solution)/shard_map/ppermute | solution.py:253
  19.7 4.6 %all-to-all-start = ((bf16[8,2,128,128]{3,2,1,0:T(8,128)(2,1)}), bf16[8,2,128,128]{3,2,1,0:T(8,128)(2,1)S(1)}, u32[]{:S(2)}, u32[]{:S(2)}) async-start(bf16[8,2,128,128]{3,2,1,0:T(8,128)(2,1)} %maximum_bitcast_fusion), calls=%async_computation | async-start | bytes 1048576 | tf_op jit(solution)/shard_map/all_to_all | solution.py:275
  25.5 2.4 %collective-permute-start.9 = (bf16[2,2,128,128]{3,2,1,0:T(8,128)(2,1)S(1)}, bf16[2,2,128,128]{3,2,1,0:T(8,128)(2,1)S(1)}, u32[]{:S(2)}, u32[]{:S(2)}) collective-permute-start(bf16[2,2,128,128]{3,2,1,0:T(8,128)(2,1)S(1)} %pad_maximum_fusion.1), channel_id=1, source_target_pairs={{0,2},{1,3},{2,0},{3,1},{4,6},{5,7},{6,4},{7,5},{8,10},{9,11},{10,... | collective-permute-start | bytes 393224 | tf_op jit(solution)/shard_map/ppermute | solution.py:253
  28.0 5.3 %all-to-all-done.refs_2_ = bf16[8,2,128,128]{3,2,1,0:T(8,128)(2,1)S(1)} async-done(((bf16[8,2,128,128]{3,2,1,0:T(8,128)(2,1)}), bf16[8,2,128,128]{3,2,1,0:T(8,128)(2,1)S(1)}, u32[]{:S(2)}, u32[]{:S(2)}) %all-to-all-start) | async-done | bytes 524320 | tf_op jit(solution)/shard_map/all_to_all | solution.py:275
  33.3 1.8 %shard_map.93 = (f32[2,2,8,512]{3,2,1,0:T(8,128)S(1)}, f32[2,128,512]{2,1,0:T(8,128)S(1)}) custom-call(s32[64]{0:T(128)S(1)} %copy-done, s32[5]{0:T(128)S(1)} %pad_add_fusion.refs_1_, bf16[8,2,128,128]{3,2,1,0:T(8,128)(2,1)S(1)} %all-to-all-done.refs_2_, bf16[4,2,128,128]{3,2,1,0:T(8,128)(2,1)S(1)} %constant_dynamic-update-slice_fusion.refs_3_.refs_4_, ...), custom_call_target="tpu_custom_call" | custom-call | flops 500000000 | bytes 2000000 | tf_op jit(solution)/shard_map/pallas_call | solution.py:203
  35.7 2.0 %collective-permute-start.6 = (bf16[4,2,128,128]{3,2,1,0:T(8,128)(2,1)S(1)}, bf16[4,2,128,128]{3,2,1,0:T(8,128)(2,1)S(1)}, u32[]{:S(2)}, u32[]{:S(2)}) collective-permute-start(bf16[4,2,128,128]{3,2,1,0:T(8,128)(2,1)S(1)} %collective-permute-done.4.refs_3_.refs_4_), channel_id=1, source_target_pairs={{0,4},{1,29},{2,6},{3,31},{4,8},{5,1},{6,10},{7,3},{8,12},{9,5},{1... | collective-permute-start | bytes 786440 | tf_op jit(solution)/shard_map/ppermute | solution.py:253
  37.7 2.3 %shard_map.94 = (f32[2,2,8,512]{3,2,1,0:T(8,128)S(1)}, f32[2,128,512]{2,1,0:T(8,128)S(1)}) custom-call(s32[64]{0:T(128)S(1)} %copy-done, s32[5]{0:T(128)S(1)} %pad_add_fusion.refs_1_, bf16[8,2,128,128]{3,2,1,0:T(8,128)(2,1)S(1)} %all-to-all-done.refs_2_, bf16[4,2,128,128]{3,2,1,0:T(8,128)(2,1)S(1)} %collective-permute-done.4.refs_3_.refs_4_, ...), custom_call_target="tpu_custom_call" | custom-call | flops 500000000 | bytes 2000000 | tf_op jit(solution)/shard_map/pallas_call | solution.py:203
  40.0 2.3 %shard_map.95 = (f32[2,2,8,512]{3,2,1,0:T(8,128)S(1)}, f32[2,128,512]{2,1,0:T(8,128)S(1)}) custom-call(s32[64]{0:T(128)S(1)} %copy-done, s32[5]{0:T(128)S(1)} %pad_add_fusion.refs_1_, bf16[8,2,128,128]{3,2,1,0:T(8,128)(2,1)S(1)} %all-to-all-done.refs_2_, bf16[4,2,128,128]{3,2,1,0:T(8,128)(2,1)S(1)} %collective-permute-done.7.refs_3_.refs_5_, ...), custom_call_target="tpu_custom_call" | custom-call | flops 500000000 | bytes 2000000 | tf_op jit(solution)/shard_map/pallas_call | solution.py:203
  42.4 2.0 %shard_map.96 = (f32[2,2,8,512]{3,2,1,0:T(8,128)S(1)}, bf16[8,128,128]{2,1,0:T(8,128)(2,1)S(1)}) custom-call(s32[64]{0:T(128)S(1)} %copy-done, s32[5]{0:T(128)S(1)} %pad_add_fusion.refs_1_, bf16[8,2,128,128]{3,2,1,0:T(8,128)(2,1)S(1)} %all-to-all-done.refs_2_, bf16[4,2,128,128]{3,2,1,0:T(8,128)(2,1)S(1)} %collective-permute-done.5.refs_3_.refs_4_, ...), custom_call_target="tpu_custom_call" | custom-call | flops 500000000 | bytes 2000000 | tf_op jit(solution)/shard_map/pallas_call | solution.py:203
  44.4 2.2 %shard_map.97 = (bf16[4,2,128,128]{3,2,1,0:T(8,128)(2,1)S(1)}, bf16[4,2,128,128]{3,2,1,0:T(8,128)(2,1)S(1)}, f32[2,128,512]{2,1,0:T(8,128)S(1)}) custom-call(s32[64]{0:T(128)S(1)} %copy-done, s32[5]{0:T(128)S(1)} %pad_add_fusion.refs_1_, bf16[8,2,128,128]{3,2,1,0:T(8,128)(2,1)S(1)} %all-to-all-done.refs_2_, f32[2,2,8,512]{3,2,1,0:T(8,128)S(1)} %get-tuple-element.56.refs_3_, ...), custom_call_target="tpu_custom_call" | custom-call | flops 1000000000 | bytes 2000000 | tf_op jit(solution)/shard_map/pallas_call | solution.py:203
  46.7 4.4 %collective-permute-start.10 = (bf16[4,2,128,128]{3,2,1,0:T(8,128)(2,1)S(1)}, bf16[4,2,128,128]{3,2,1,0:T(8,128)(2,1)S(1)}, u32[]{:S(2)}, u32[]{:S(2)}) collective-permute-start(bf16[4,2,128,128]{3,2,1,0:T(8,128)(2,1)S(1)} %get-tuple-element.59), channel_id=1, source_target_pairs={{0,1},{1,0},{2,3},{3,2},{4,5},{5,4},{6,7},{7,6},{8,9},{9,8},{10,11... | collective-permute-start | bytes 786440 | tf_op jit(solution)/shard_map/ppermute | solution.py:253
  51.1 1.5 %shard_map.98 = (bf16[4,2,128,128]{3,2,1,0:T(8,128)(2,1)S(1)}, bf16[4,2,128,128]{3,2,1,0:T(8,128)(2,1)S(1)}, f32[2,128,512]{2,1,0:T(8,128)S(1)}) custom-call(s32[64]{0:T(128)S(1)} %copy-done, s32[5]{0:T(128)S(1)} %pad_add_fusion.refs_1_, bf16[8,2,128,128]{3,2,1,0:T(8,128)(2,1)S(1)} %all-to-all-done.refs_2_, f32[2,2,8,512]{3,2,1,0:T(8,128)S(1)} %get-tuple-element.56.refs_3_, ...), custom_call_target="tpu_custom_call" | custom-call | flops 1000000000 | bytes 2000000 | tf_op jit(solution)/shard_map/pallas_call | solution.py:203
  52.6 2.6 %shard_map.99 = (bf16[4,2,128,128]{3,2,1,0:T(8,128)(2,1)S(1)}, bf16[4,2,128,128]{3,2,1,0:T(8,128)(2,1)S(1)}, f32[2,128,512]{2,1,0:T(8,128)S(1)}) custom-call(s32[64]{0:T(128)S(1)} %copy-done, s32[5]{0:T(128)S(1)} %pad_add_fusion.refs_1_, bf16[8,2,128,128]{3,2,1,0:T(8,128)(2,1)S(1)} %all-to-all-done.refs_2_, f32[2,2,8,512]{3,2,1,0:T(8,128)S(1)} %get-tuple-element.56.refs_3_, ...), custom_call_target="tpu_custom_call" | custom-call | flops 1000000000 | bytes 2000000 | tf_op jit(solution)/shard_map/pallas_call | solution.py:203
  55.4 3.5 %collective-permute-start.15 = (bf16[4,2,128,128]{3,2,1,0:T(8,128)(2,1)S(1)}, bf16[4,2,128,128]{3,2,1,0:T(8,128)(2,1)S(1)}, u32[]{:S(2)}, u32[]{:S(2)}) collective-permute-start(bf16[4,2,128,128]{3,2,1,0:T(8,128)(2,1)S(1)} %get-tuple-element.74), channel_id=1, source_target_pairs={{0,1},{1,0},{2,3},{3,2},{4,5},{5,4},{6,7},{7,6},{8,9},{9,8},{10,11... | collective-permute-start | bytes 786440 | tf_op jit(solution)/shard_map/ppermute | solution.py:253
  58.9 3.4 %shard_map.100 = (bf16[4,2,128,128]{3,2,1,0:T(8,128)(2,1)S(1)}, bf16[4,2,128,128]{3,2,1,0:T(8,128)(2,1)S(1)}, bf16[8,2,128,128]{3,2,1,0:T(8,128)(2,1)}) custom-call(s32[64]{0:T(128)S(1)} %copy-done, s32[5]{0:T(128)S(1)} %pad_add_fusion.refs_1_, bf16[8,2,128,128]{3,2,1,0:T(8,128)(2,1)S(1)} %all-to-all-done.refs_2_, ...), custom_call_target="tpu_custom_call" | custom-call | flops 1000000000 | bytes 2000000 | tf_op jit(solution)/shard_map/pallas_call | solution.py:203
  63.0 3.5 %all-to-all-start.1 = ((bf16[8,2,128,128]{3,2,1,0:T(8,128)(2,1)}), bf16[8,2,128,128]{3,2,1,0:T(8,128)(2,1)S(1)}, u32[]{:S(2)}, u32[]{:S(2)}) async-start(bf16[8,2,128,128]{3,2,1,0:T(8,128)(2,1)} %get-tuple-element.76), calls=%async_computation.1 | async-start | bytes 1048576 | tf_op jit(solution)/shard_map/all_to_all | solution.py:306
  66.6 3.5 %collective-permute-done.16 = bf16[4,2,128,128]{3,2,1,0:T(8,128)(2,1)S(1)} collective-permute-done((bf16[4,2,128,128]{3,2,1,0:T(8,128)(2,1)S(1)}, bf16[4,2,128,128]{3,2,1,0:T(8,128)(2,1)S(1)}, u32[]{:S(2)}, u32[]{:S(2)}) %collective-permute-start.16) | collective-permute-done | bytes 262176 | tf_op jit(solution)/shard_map/ppermute | solution.py:253
  70.4 1.4 %collective-permute-start.18 = (bf16[2,2,128,128]{3,2,1,0:T(8,128)(2,1)S(1)}, bf16[2,2,128,128]{3,2,1,0:T(8,128)(2,1)S(1)}, u32[]{:S(2)}, u32[]{:S(2)}) collective-permute-start(bf16[2,2,128,128]{3,2,1,0:T(8,128)(2,1)S(1)} %get-tuple-element.91), channel_id=1, source_target_pairs={{0,30},{1,5},{2,28},{3,7},{4,2},{5,9},{6,0},{7,11},{8,6},{9,13},{1... | collective-permute-start | bytes 393224 | tf_op jit(solution)/shard_map/ppermute | solution.py:253
  71.7 2.6 %collective-permute-done.13 = bf16[2,2,128,128]{3,2,1,0:T(8,128)(2,1)S(1)} collective-permute-done((bf16[2,2,128,128]{3,2,1,0:T(8,128)(2,1)S(1)}, bf16[2,2,128,128]{3,2,1,0:T(8,128)(2,1)S(1)}, u32[]{:S(2)}, u32[]{:S(2)}) %collective-permute-start.13) | collective-permute-done | bytes 131104 | tf_op jit(solution)/shard_map/ppermute | solution.py:253
  74.4 3.5 %collective-permute-done.17 = bf16[2,2,128,128]{3,2,1,0:T(8,128)(2,1)S(1)} collective-permute-done((bf16[2,2,128,128]{3,2,1,0:T(8,128)(2,1)S(1)}, bf16[2,2,128,128]{3,2,1,0:T(8,128)(2,1)S(1)}, u32[]{:S(2)}, u32[]{:S(2)}) %collective-permute-start.17) | collective-permute-done | bytes 131104 | tf_op jit(solution)/shard_map/ppermute | solution.py:253
  78.4 4.0 %collective-permute-start.19 = (bf16[2,128,128]{2,1,0:T(8,128)(2,1)S(1)}, bf16[2,128,128]{2,1,0:T(8,128)(2,1)S(1)}, u32[]{:S(2)}, u32[]{:S(2)}) collective-permute-start(bf16[2,128,128]{2,1,0:T(8,128)(2,1)S(1)} %fusion.1), channel_id=1, source_target_pairs={{0,1},{1,0},{2,3},{3,2},{4,5},{5,4},{6,7},{7,6},{8,9},{9,8},{10,11... | collective-permute-start | bytes 196616 | tf_op jit(solution)/shard_map/ppermute | solution.py:253
  (63 shorter events, 10.9 us)
Async XLA Ops:
  0.6 12.4 %copy-start.1 = (bf16[128,1024]{1,0:T(8,128)(2,1)S(1)}, bf16[128,1024]{1,0:T(8,128)(2,1)}, u32[]{:S(2)}) copy-start(bf16[128,1024]{1,0:T(8,128)(2,1)} %param.6) | copy-start | bytes 786436
  1.5 4.2 %collective-permute-start = (bf16[2,128,128]{2,1,0:T(8,128)(2,1)S(1)}, bf16[2,128,128]{2,1,0:T(8,128)(2,1)S(1)}, u32[]{:S(2)}, u32[]{:S(2)}) collective-permute-start(bf16[2,128,128]{2,1,0:T(8,128)(2,1)S(1)} %get-tuple-element.95), channel_id=1, source_target_pairs={{0,1},{1,0},{2,3},{3,2},{4,5},{5,4},{6,7},{7,6},{8,9},{9,8},{10,11... | collective-permute-start | bytes 196616 | tf_op jit(solution)/shard_map/ppermute | solution.py:253
  5.7 8.8 %collective-permute-start.1 = (bf16[2,2,128,128]{3,2,1,0:T(8,128)(2,1)S(1)}, bf16[2,2,128,128]{3,2,1,0:T(8,128)(2,1)S(1)}, u32[]{:S(2)}, u32[]{:S(2)}) collective-permute-start(bf16[2,2,128,128]{3,2,1,0:T(8,128)(2,1)S(1)} %pad_maximum_fusion.1), channel_id=1, source_target_pairs={{0,4},{1,31},{2,6},{3,29},{4,8},{5,3},{6,10},{7,1},{8,12},{9,7},{1... | collective-permute-start | bytes 393224 | tf_op jit(solution)/shard_map/ppermute | solution.py:253
  12.3 4.1 %collective-permute-start.2 = (bf16[2,2,128,128]{3,2,1,0:T(8,128)(2,1)S(1)}, bf16[2,2,128,128]{3,2,1,0:T(8,128)(2,1)S(1)}, u32[]{:S(2)}, u32[]{:S(2)}) collective-permute-start(bf16[2,2,128,128]{3,2,1,0:T(8,128)(2,1)S(1)} %pad_maximum_fusion.1), channel_id=1, source_target_pairs={{0,6},{1,29},{2,4},{3,31},{4,10},{5,1},{6,8},{7,3},{8,14},{9,5},{1... | collective-permute-start | bytes 393224 | tf_op jit(solution)/shard_map/ppermute | solution.py:253
  16.4 7.8 %collective-permute-start.3 = (bf16[4,2,128,128]{3,2,1,0:T(8,128)(2,1)S(1)}, bf16[4,2,128,128]{3,2,1,0:T(8,128)(2,1)S(1)}, u32[]{:S(2)}, u32[]{:S(2)}) collective-permute-start(bf16[4,2,128,128]{3,2,1,0:T(8,128)(2,1)S(1)} %constant_dynamic-update-slice_fusion.refs_3_.refs_4_), channel_id=1, source_target_pairs={{0,4},{1,29},{2,6},{3,31},{4,8},{5,1},{6,10},{7,3},{8,12},{9,5},{1... | collective-permute-start | bytes 786440 | tf_op jit(solution)/shard_map/ppermute | solution.py:253
  19.7 13.6 %all-to-all-start = ((bf16[8,2,128,128]{3,2,1,0:T(8,128)(2,1)}), bf16[8,2,128,128]{3,2,1,0:T(8,128)(2,1)S(1)}, u32[]{:S(2)}, u32[]{:S(2)}) async-start(bf16[8,2,128,128]{3,2,1,0:T(8,128)(2,1)} %maximum_bitcast_fusion), calls=%async_computation | async-start | bytes 1048576 | tf_op jit(solution)/shard_map/all_to_all | solution.py:275
  24.3 10.8 %collective-permute-start.4 = (bf16[4,2,128,128]{3,2,1,0:T(8,128)(2,1)S(1)}, bf16[4,2,128,128]{3,2,1,0:T(8,128)(2,1)S(1)}, u32[]{:S(2)}, u32[]{:S(2)}) collective-permute-start(bf16[4,2,128,128]{3,2,1,0:T(8,128)(2,1)S(1)} %collective-permute-done.3.refs_4_), channel_id=1, source_target_pairs={{0,4},{1,29},{2,6},{3,31},{4,8},{5,1},{6,10},{7,3},{8,12},{9,5},{1... | collective-permute-start | bytes 786440 | tf_op jit(solution)/shard_map/ppermute | solution.py:253
  25.5 7.8 %copy-start = (s32[64]{0:T(128)S(1)}, s32[64]{0:T(128)}, u32[]{:S(2)}) copy-start(s32[64]{0:T(128)} %refs_0_.15) | copy-start | bytes 772
  25.5 12.1 %collective-permute-start.9 = (bf16[2,2,128,128]{3,2,1,0:T(8,128)(2,1)S(1)}, bf16[2,2,128,128]{3,2,1,0:T(8,128)(2,1)S(1)}, u32[]{:S(2)}, u32[]{:S(2)}) collective-permute-start(bf16[2,2,128,128]{3,2,1,0:T(8,128)(2,1)S(1)} %pad_maximum_fusion.1), channel_id=1, source_target_pairs={{0,2},{1,3},{2,0},{3,1},{4,6},{5,7},{6,4},{7,5},{8,10},{9,11},{10,... | collective-permute-start | bytes 393224 | tf_op jit(solution)/shard_map/ppermute | solution.py:253
  35.1 4.9 %collective-permute-start.7 = (bf16[4,2,128,128]{3,2,1,0:T(8,128)(2,1)S(1)}, bf16[4,2,128,128]{3,2,1,0:T(8,128)(2,1)S(1)}, u32[]{:S(2)}, u32[]{:S(2)}) collective-permute-start(bf16[4,2,128,128]{3,2,1,0:T(8,128)(2,1)S(1)} %constant_dynamic-update-slice_fusion.refs_3_.refs_4_), channel_id=1, source_target_pairs={{0,1},{1,0},{2,3},{3,2},{4,5},{5,4},{6,7},{7,6},{8,9},{9,8},{10,11... | collective-permute-start | bytes 786440 | tf_op jit(solution)/shard_map/ppermute | solution.py:253
  35.4 4.7 %collective-permute-start.8 = (bf16[4,2,128,128]{3,2,1,0:T(8,128)(2,1)S(1)}, bf16[4,2,128,128]{3,2,1,0:T(8,128)(2,1)S(1)}, u32[]{:S(2)}, u32[]{:S(2)}) collective-permute-start(bf16[4,2,128,128]{3,2,1,0:T(8,128)(2,1)S(1)} %collective-permute-done.3.refs_4_), channel_id=1, source_target_pairs={{0,1},{1,0},{2,3},{3,2},{4,5},{5,4},{6,7},{7,6},{8,9},{9,8},{10,11... | collective-permute-start | bytes 786440 | tf_op jit(solution)/shard_map/ppermute | solution.py:253
  35.7 6.7 %collective-permute-start.6 = (bf16[4,2,128,128]{3,2,1,0:T(8,128)(2,1)S(1)}, bf16[4,2,128,128]{3,2,1,0:T(8,128)(2,1)S(1)}, u32[]{:S(2)}, u32[]{:S(2)}) collective-permute-start(bf16[4,2,128,128]{3,2,1,0:T(8,128)(2,1)S(1)} %collective-permute-done.4.refs_3_.refs_4_), channel_id=1, source_target_pairs={{0,4},{1,29},{2,6},{3,31},{4,8},{5,1},{6,10},{7,3},{8,12},{9,5},{1... | collective-permute-start | bytes 786440 | tf_op jit(solution)/shard_map/ppermute | solution.py:253
  37.7 4.7 %collective-permute-start.5 = (bf16[4,2,128,128]{3,2,1,0:T(8,128)(2,1)S(1)}, bf16[4,2,128,128]{3,2,1,0:T(8,128)(2,1)S(1)}, u32[]{:S(2)}, u32[]{:S(2)}) collective-permute-start(bf16[4,2,128,128]{3,2,1,0:T(8,128)(2,1)S(1)} %collective-permute-done.4.refs_3_.refs_4_), channel_id=1, source_target_pairs={{0,1},{1,0},{2,3},{3,2},{4,5},{5,4},{6,7},{7,6},{8,9},{9,8},{10,11... | collective-permute-start | bytes 786440 | tf_op jit(solution)/shard_map/ppermute | solution.py:253
  46.6 8.5 %collective-permute-start.11 = (bf16[4,2,128,128]{3,2,1,0:T(8,128)(2,1)S(1)}, bf16[4,2,128,128]{3,2,1,0:T(8,128)(2,1)S(1)}, u32[]{:S(2)}, u32[]{:S(2)}) collective-permute-start(bf16[4,2,128,128]{3,2,1,0:T(8,128)(2,1)S(1)} %get-tuple-element.60), channel_id=1, source_target_pairs={{0,28},{1,5},{2,30},{3,7},{4,0},{5,9},{6,2},{7,11},{8,4},{9,13},{1... | collective-permute-start | bytes 786440 | tf_op jit(solution)/shard_map/ppermute | solution.py:253
  46.7 8.4 %collective-permute-start.10 = (bf16[4,2,128,128]{3,2,1,0:T(8,128)(2,1)S(1)}, bf16[4,2,128,128]{3,2,1,0:T(8,128)(2,1)S(1)}, u32[]{:S(2)}, u32[]{:S(2)}) collective-permute-start(bf16[4,2,128,128]{3,2,1,0:T(8,128)(2,1)S(1)} %get-tuple-element.59), channel_id=1, source_target_pairs={{0,1},{1,0},{2,3},{3,2},{4,5},{5,4},{6,7},{7,6},{8,9},{9,8},{10,11... | collective-permute-start | bytes 786440 | tf_op jit(solution)/shard_map/ppermute | solution.py:253
  55.3 7.0 %collective-permute-start.12 = (bf16[4,2,128,128]{3,2,1,0:T(8,128)(2,1)S(1)}, bf16[4,2,128,128]{3,2,1,0:T(8,128)(2,1)S(1)}, u32[]{:S(2)}, u32[]{:S(2)}) collective-permute-start(bf16[4,2,128,128]{3,2,1,0:T(8,128)(2,1)S(1)} %add_convert_fusion.2), channel_id=1, source_target_pairs={{0,28},{1,5},{2,30},{3,7},{4,0},{5,9},{6,2},{7,11},{8,4},{9,13},{1... | collective-permute-start | bytes 786440 | tf_op jit(solution)/shard_map/ppermute | solution.py:253
  55.4 7.4 %collective-permute-start.15 = (bf16[4,2,128,128]{3,2,1,0:T(8,128)(2,1)S(1)}, bf16[4,2,128,128]{3,2,1,0:T(8,128)(2,1)S(1)}, u32[]{:S(2)}, u32[]{:S(2)}) collective-permute-start(bf16[4,2,128,128]{3,2,1,0:T(8,128)(2,1)S(1)} %get-tuple-element.74), channel_id=1, source_target_pairs={{0,1},{1,0},{2,3},{3,2},{4,5},{5,4},{6,7},{7,6},{8,9},{9,8},{10,11... | collective-permute-start | bytes 786440 | tf_op jit(solution)/shard_map/ppermute | solution.py:253
  62.3 4.4 %collective-permute-start.14 = (bf16[4,2,128,128]{3,2,1,0:T(8,128)(2,1)S(1)}, bf16[4,2,128,128]{3,2,1,0:T(8,128)(2,1)S(1)}, u32[]{:S(2)}, u32[]{:S(2)}) collective-permute-start(bf16[4,2,128,128]{3,2,1,0:T(8,128)(2,1)S(1)} %get-tuple-element.72), channel_id=1, source_target_pairs={{0,1},{1,0},{2,3},{3,2},{4,5},{5,4},{6,7},{7,6},{8,9},{9,8},{10,11... | collective-permute-start | bytes 786440 | tf_op jit(solution)/shard_map/ppermute | solution.py:253
  62.9 7.3 %collective-permute-start.16 = (bf16[4,2,128,128]{3,2,1,0:T(8,128)(2,1)S(1)}, bf16[4,2,128,128]{3,2,1,0:T(8,128)(2,1)S(1)}, u32[]{:S(2)}, u32[]{:S(2)}) collective-permute-start(bf16[4,2,128,128]{3,2,1,0:T(8,128)(2,1)S(1)} %add_convert_fusion.1), channel_id=1, source_target_pairs={{0,28},{1,5},{2,30},{3,7},{4,0},{5,9},{6,2},{7,11},{8,4},{9,13},{1... | collective-permute-start | bytes 786440 | tf_op jit(solution)/shard_map/ppermute | solution.py:253
  63.0 15.0 %all-to-all-start.1 = ((bf16[8,2,128,128]{3,2,1,0:T(8,128)(2,1)}), bf16[8,2,128,128]{3,2,1,0:T(8,128)(2,1)S(1)}, u32[]{:S(2)}, u32[]{:S(2)}) async-start(bf16[8,2,128,128]{3,2,1,0:T(8,128)(2,1)} %get-tuple-element.76), calls=%async_computation.1 | async-start | bytes 1048576 | tf_op jit(solution)/shard_map/all_to_all | solution.py:306
  66.5 7.8 %collective-permute-start.13 = (bf16[2,2,128,128]{3,2,1,0:T(8,128)(2,1)S(1)}, bf16[2,2,128,128]{3,2,1,0:T(8,128)(2,1)S(1)}, u32[]{:S(2)}, u32[]{:S(2)}) collective-permute-start(bf16[2,2,128,128]{3,2,1,0:T(8,128)(2,1)S(1)} %slice.34), channel_id=1, source_target_pairs={{0,2},{1,3},{2,0},{3,1},{4,6},{5,7},{6,4},{7,5},{8,10},{9,11},{10,... | collective-permute-start | bytes 393224 | tf_op jit(solution)/shard_map/ppermute | solution.py:253
  70.3 7.6 %collective-permute-start.17 = (bf16[2,2,128,128]{3,2,1,0:T(8,128)(2,1)S(1)}, bf16[2,2,128,128]{3,2,1,0:T(8,128)(2,1)S(1)}, u32[]{:S(2)}, u32[]{:S(2)}) collective-permute-start(bf16[2,2,128,128]{3,2,1,0:T(8,128)(2,1)S(1)} %get-tuple-element.90), channel_id=1, source_target_pairs={{0,28},{1,7},{2,30},{3,5},{4,0},{5,11},{6,2},{7,9},{8,4},{9,15},{1... | collective-permute-start | bytes 393224 | tf_op jit(solution)/shard_map/ppermute | solution.py:253
  70.4 7.5 %collective-permute-start.18 = (bf16[2,2,128,128]{3,2,1,0:T(8,128)(2,1)S(1)}, bf16[2,2,128,128]{3,2,1,0:T(8,128)(2,1)S(1)}, u32[]{:S(2)}, u32[]{:S(2)}) collective-permute-start(bf16[2,2,128,128]{3,2,1,0:T(8,128)(2,1)S(1)} %get-tuple-element.91), channel_id=1, source_target_pairs={{0,30},{1,5},{2,28},{3,7},{4,2},{5,9},{6,0},{7,11},{8,6},{9,13},{1... | collective-permute-start | bytes 393224 | tf_op jit(solution)/shard_map/ppermute | solution.py:253
  78.4 5.7 %collective-permute-start.19 = (bf16[2,128,128]{2,1,0:T(8,128)(2,1)S(1)}, bf16[2,128,128]{2,1,0:T(8,128)(2,1)S(1)}, u32[]{:S(2)}, u32[]{:S(2)}) collective-permute-start(bf16[2,128,128]{2,1,0:T(8,128)(2,1)S(1)} %fusion.1), channel_id=1, source_target_pairs={{0,1},{1,0},{2,3},{3,2},{4,5},{5,4},{6,7},{7,6},{8,9},{9,8},{10,11... | collective-permute-start | bytes 196616 | tf_op jit(solution)/shard_map/ppermute | solution.py:253
  (2 other events, 6.6 us)

commit v3 on v2

--- a/solution.py
+++ b/solution.py
@@ -273,13 +273,14 @@
     own = jnp.concatenate([pair, send(pair, TWIN)])
     qd = jnp.stack([queries.reshape(rows, GROUP, HEAD), output_gradient.reshape(rows, GROUP, HEAD)])
     qd = lax.all_to_all(jnp.transpose(qd, (2, 0, 1, 3)), "head", 0, 0, tiled=True)
+    segment_ids, qd = after(segment_ids, qd)
     starts = jnp.sum(segment_ids[None, :] < jnp.arange(1, 4, dtype=jnp.int32)[:, None], axis=1)
     place = jnp.stack([lax.axis_index("inner"), lax.axis_index("outer")])
     meta = jnp.concatenate([place.astype(jnp.int32), starts.astype(jnp.int32)])
 
-    run = functools.partial(forward, block_perm, meta, qd)
     near2 = send(near1, ONWARD)
     near3 = send(near2, ONWARD)
+    run = functools.partial(forward, block_perm, meta, qd)
     state = run((("near", 1), ("near", 2)), (near1, near2), None, False)
     near3, near1, near2, *state = after(near3, near1, near2, *state)
     near4 = send(near3, ONWARD)

time: 85.5 us -> 84.3 us (0.986)
  waiting for transfers between devices: 17.7 us -> 16.2 us
    ppermute x20, waiting for transfers between devices: 12.5 us -> 10 us  [send(): return lax.ppermute(x, AXES, pairs)]
    all_to_all x1, waiting for transfers between devices: 5.28 us -> 6.21 us  [on_device(): lax.all_to_all(jnp.transpose(qd, (2, 0, 1, 3)), 'head', 0, 0, tiled=True)]
where the time goes in v3:
time: 84.3 us; the launch traced here: 83.3 us
  starting transfers between devices  41.3 us (49%)
  Pallas kernels  17.6 us (21%)
  waiting for transfers between devices  16.2 us (19%)
  local copies, waits for them, and re-layouts  4.84 us (6%)
  other arithmetic  2.41 us (3%)
  between operations  0.93 us (1%)
    ppermute x20, starting transfers between devices, send(): return lax.ppermute(x, AXES, pairs)  33.5 us
    pallas_call x8, Pallas kernels, call(): pl.pallas_call(kernel, out_shape=outs, in_specs=[SMEM, SMEM] + [VMEM] * (...  17.6 us
    ppermute x20, waiting for transfers between devices, send(): return lax.ppermute(x, AXES, pairs)  10 us
    all_to_all x1, waiting for transfers between devices, on_device(): lax.all_to_all(jnp.transpose(qd, (2, 0, 1, 3)), 'head', 0, 0, tiled=True)  6.21 us
    all_to_all x1, starting transfers between devices, on_device(): lax.all_to_all(jnp.transpose(qd, (2, 0, 1, 3)), 'head', 0, 0, tiled=True)  4.13 us
    all_to_all x1, starting transfers between devices, on_device(): back = lax.all_to_all(back, 'head', 0, 0, tiled=True)  3.66 us
    unnamed x13, local copies, waits for them, and re-layouts  3.39 us
  transfers between devices with their start and end apart: 22, of which 6 were waited for; matrix products, arithmetic and copies ran while one was open for 5% of the time, Pallas kernels for 16%

profile of v3, /device:TPU:1, one launch (start us, length us, event | category | flops | bytes accessed | tf_op | source)
XLA Modules:
  0.0 83.3 jit_solution(11001259896644572734)
XLA Ops:
  1.5 3.3 %collective-permute-start = (bf16[2,128,128]{2,1,0:T(8,128)(2,1)S(1)}, bf16[2,128,128]{2,1,0:T(8,128)(2,1)S(1)}, u32[]{:S(2)}, u32[]{:S(2)}) collective-permute-start(bf16[2,128,128]{2,1,0:T(8,128)(2,1)S(1)} %get-tuple-element.99), channel_id=1, source_target_pairs={{0,1},{1,0},{2,3},{3,2},{4,5},{5,4},{6,7},{7,6},{8,9},{9,8},{10,11... | collective-permute-start | bytes 196616 | tf_op jit(solution)/shard_map/ppermute | solution.py:253
  5.7 6.5 %collective-permute-start.1 = (bf16[2,2,128,128]{3,2,1,0:T(8,128)(2,1)S(1)}, bf16[2,2,128,128]{3,2,1,0:T(8,128)(2,1)S(1)}, u32[]{:S(2)}, u32[]{:S(2)}) collective-permute-start(bf16[2,2,128,128]{3,2,1,0:T(8,128)(2,1)S(1)} %pad_maximum_fusion.1), channel_id=1, source_target_pairs={{0,4},{1,31},{2,6},{3,29},{4,8},{5,3},{6,10},{7,1},{8,12},{9,7},{1... | collective-permute-start | bytes 393224 | tf_op jit(solution)/shard_map/ppermute | solution.py:253
  15.4 4.1 %all-to-all-start = ((bf16[8,2,128,128]{3,2,1,0:T(8,128)(2,1)}), bf16[8,2,128,128]{3,2,1,0:T(8,128)(2,1)S(1)}, u32[]{:S(2)}, u32[]{:S(2)}) async-start(bf16[8,2,128,128]{3,2,1,0:T(8,128)(2,1)} %maximum_bitcast_fusion), calls=%async_computation | async-start | bytes 1048576 | tf_op jit(solution)/shard_map/all_to_all | solution.py:275
  20.4 1.6 %collective-permute-start.9 = (bf16[2,2,128,128]{3,2,1,0:T(8,128)(2,1)S(1)}, bf16[2,2,128,128]{3,2,1,0:T(8,128)(2,1)S(1)}, u32[]{:S(2)}, u32[]{:S(2)}) collective-permute-start(bf16[2,2,128,128]{3,2,1,0:T(8,128)(2,1)S(1)} %pad_maximum_fusion.1), channel_id=1, source_target_pairs={{0,2},{1,3},{2,0},{3,1},{4,6},{5,7},{6,4},{7,5},{8,10},{9,11},{10,... | collective-permute-start | bytes 393224 | tf_op jit(solution)/shard_map/ppermute | solution.py:253
  22.0 6.2 %all-to-all-done.refs_2_ = bf16[8,2,128,128]{3,2,1,0:T(8,128)(2,1)S(1)} async-done(((bf16[8,2,128,128]{3,2,1,0:T(8,128)(2,1)}), bf16[8,2,128,128]{3,2,1,0:T(8,128)(2,1)S(1)}, u32[]{:S(2)}, u32[]{:S(2)}) %all-to-all-start) | async-done | bytes 524320 | tf_op jit(solution)/shard_map/all_to_all | solution.py:275
  30.1 1.8 %shard_map.93 = (f32[2,2,8,512]{3,2,1,0:T(8,128)S(1)}, f32[2,128,512]{2,1,0:T(8,128)S(1)}) custom-call(s32[64]{0:T(128)S(1)} %copy-done, s32[5]{0:T(128)S(1)} %pad_add_fusion.refs_1_, bf16[8,2,128,128]{3,2,1,0:T(8,128)(2,1)S(1)} %all-to-all-done.refs_2_, bf16[4,2,128,128]{3,2,1,0:T(8,128)(2,1)S(1)} %constant_dynamic-update-slice_fusion.refs_3_.refs_4_, ...), custom_call_target="tpu_custom_call" | custom-call | flops 500000000 | bytes 2000000 | tf_op jit(solution)/shard_map/pallas_call | solution.py:203
  31.9 2.0 %collective-permute-done.4.refs_3_.refs_4_ = bf16[4,2,128,128]{3,2,1,0:T(8,128)(2,1)S(1)} collective-permute-done((bf16[4,2,128,128]{3,2,1,0:T(8,128)(2,1)S(1)}, bf16[4,2,128,128]{3,2,1,0:T(8,128)(2,1)S(1)}, u32[]{:S(2)}, u32[]{:S(2)}) %collective-permute-start.4) | collective-permute-done | bytes 262176 | tf_op jit(solution)/shard_map/ppermute | solution.py:253
  33.9 1.3 %collective-permute-start.7 = (bf16[4,2,128,128]{3,2,1,0:T(8,128)(2,1)S(1)}, bf16[4,2,128,128]{3,2,1,0:T(8,128)(2,1)S(1)}, u32[]{:S(2)}, u32[]{:S(2)}) collective-permute-start(bf16[4,2,128,128]{3,2,1,0:T(8,128)(2,1)S(1)} %constant_dynamic-update-slice_fusion.refs_3_.refs_4_), channel_id=1, source_target_pairs={{0,1},{1,0},{2,3},{3,2},{4,5},{5,4},{6,7},{7,6},{8,9},{9,8},{10,11... | collective-permute-start | bytes 786440 | tf_op jit(solution)/shard_map/ppermute | solution.py:253
  37.0 2.3 %shard_map.94 = (f32[2,2,8,512]{3,2,1,0:T(8,128)S(1)}, f32[2,128,512]{2,1,0:T(8,128)S(1)}) custom-call(s32[64]{0:T(128)S(1)} %copy-done, s32[5]{0:T(128)S(1)} %pad_add_fusion.refs_1_, bf16[8,2,128,128]{3,2,1,0:T(8,128)(2,1)S(1)} %all-to-all-done.refs_2_, bf16[4,2,128,128]{3,2,1,0:T(8,128)(2,1)S(1)} %collective-permute-done.4.refs_3_.refs_4_, ...), custom_call_target="tpu_custom_call" | custom-call | flops 500000000 | bytes 2000000 | tf_op jit(solution)/shard_map/pallas_call | solution.py:203
  39.4 1.8 %shard_map.95 = (f32[2,2,8,512]{3,2,1,0:T(8,128)S(1)}, f32[2,128,512]{2,1,0:T(8,128)S(1)}) custom-call(s32[64]{0:T(128)S(1)} %copy-done, s32[5]{0:T(128)S(1)} %pad_add_fusion.refs_1_, bf16[8,2,128,128]{3,2,1,0:T(8,128)(2,1)S(1)} %all-to-all-done.refs_2_, bf16[4,2,128,128]{3,2,1,0:T(8,128)(2,1)S(1)} %collective-permute-done.7.refs_3_.refs_5_, ...), custom_call_target="tpu_custom_call" | custom-call | flops 500000000 | bytes 2000000 | tf_op jit(solution)/shard_map/pallas_call | solution.py:203
  41.2 2.0 %shard_map.96 = (f32[2,2,8,512]{3,2,1,0:T(8,128)S(1)}, bf16[8,128,128]{2,1,0:T(8,128)(2,1)S(1)}) custom-call(s32[64]{0:T(128)S(1)} %copy-done, s32[5]{0:T(128)S(1)} %pad_add_fusion.refs_1_, bf16[8,2,128,128]{3,2,1,0:T(8,128)(2,1)S(1)} %all-to-all-done.refs_2_, bf16[4,2,128,128]{3,2,1,0:T(8,128)(2,1)S(1)} %collective-permute-done.5.refs_3_.refs_4_, ...), custom_call_target="tpu_custom_call" | custom-call | flops 500000000 | bytes 2000000 | tf_op jit(solution)/shard_map/pallas_call | solution.py:203
  43.3 2.2 %shard_map.97 = (bf16[4,2,128,128]{3,2,1,0:T(8,128)(2,1)S(1)}, bf16[4,2,128,128]{3,2,1,0:T(8,128)(2,1)S(1)}, f32[2,128,512]{2,1,0:T(8,128)S(1)}) custom-call(s32[64]{0:T(128)S(1)} %copy-done, s32[5]{0:T(128)S(1)} %pad_add_fusion.refs_1_, bf16[8,2,128,128]{3,2,1,0:T(8,128)(2,1)S(1)} %all-to-all-done.refs_2_, f32[2,2,8,512]{3,2,1,0:T(8,128)S(1)} %get-tuple-element.60.refs_3_, ...), custom_call_target="tpu_custom_call" | custom-call | flops 1000000000 | bytes 2000000 | tf_op jit(solution)/shard_map/pallas_call | solution.py:203
  46.1 2.5 %collective-permute-start.10 = (bf16[4,2,128,128]{3,2,1,0:T(8,128)(2,1)S(1)}, bf16[4,2,128,128]{3,2,1,0:T(8,128)(2,1)S(1)}, u32[]{:S(2)}, u32[]{:S(2)}) collective-permute-start(bf16[4,2,128,128]{3,2,1,0:T(8,128)(2,1)S(1)} %get-tuple-element.63), channel_id=1, source_target_pairs={{0,1},{1,0},{2,3},{3,2},{4,5},{5,4},{6,7},{7,6},{8,9},{9,8},{10,11... | collective-permute-start | bytes 786440 | tf_op jit(solution)/shard_map/ppermute | solution.py:253
  48.6 2.5 %shard_map.98 = (bf16[4,2,128,128]{3,2,1,0:T(8,128)(2,1)S(1)}, bf16[4,2,128,128]{3,2,1,0:T(8,128)(2,1)S(1)}, f32[2,128,512]{2,1,0:T(8,128)S(1)}) custom-call(s32[64]{0:T(128)S(1)} %copy-done, s32[5]{0:T(128)S(1)} %pad_add_fusion.refs_1_, bf16[8,2,128,128]{3,2,1,0:T(8,128)(2,1)S(1)} %all-to-all-done.refs_2_, f32[2,2,8,512]{3,2,1,0:T(8,128)S(1)} %get-tuple-element.60.refs_3_, ...), custom_call_target="tpu_custom_call" | custom-call | flops 1000000000 | bytes 2000000 | tf_op jit(solution)/shard_map/pallas_call | solution.py:203
  51.1 2.0 %shard_map.99 = (bf16[4,2,128,128]{3,2,1,0:T(8,128)(2,1)S(1)}, bf16[4,2,128,128]{3,2,1,0:T(8,128)(2,1)S(1)}, f32[2,128,512]{2,1,0:T(8,128)S(1)}) custom-call(s32[64]{0:T(128)S(1)} %copy-done, s32[5]{0:T(128)S(1)} %pad_add_fusion.refs_1_, bf16[8,2,128,128]{3,2,1,0:T(8,128)(2,1)S(1)} %all-to-all-done.refs_2_, f32[2,2,8,512]{3,2,1,0:T(8,128)S(1)} %get-tuple-element.60.refs_3_, ...), custom_call_target="tpu_custom_call" | custom-call | flops 1000000000 | bytes 2000000 | tf_op jit(solution)/shard_map/pallas_call | solution.py:203
  53.4 3.0 %collective-permute-start.15 = (bf16[4,2,128,128]{3,2,1,0:T(8,128)(2,1)S(1)}, bf16[4,2,128,128]{3,2,1,0:T(8,128)(2,1)S(1)}, u32[]{:S(2)}, u32[]{:S(2)}) collective-permute-start(bf16[4,2,128,128]{3,2,1,0:T(8,128)(2,1)S(1)} %get-tuple-element.78), channel_id=1, source_target_pairs={{0,1},{1,0},{2,3},{3,2},{4,5},{5,4},{6,7},{7,6},{8,9},{9,8},{10,11... | collective-permute-start | bytes 786440 | tf_op jit(solution)/shard_map/ppermute | solution.py:253
  56.3 2.8 %shard_map.100 = (bf16[4,2,128,128]{3,2,1,0:T(8,128)(2,1)S(1)}, bf16[4,2,128,128]{3,2,1,0:T(8,128)(2,1)S(1)}, bf16[8,2,128,128]{3,2,1,0:T(8,128)(2,1)}) custom-call(s32[64]{0:T(128)S(1)} %copy-done, s32[5]{0:T(128)S(1)} %pad_add_fusion.refs_1_, bf16[8,2,128,128]{3,2,1,0:T(8,128)(2,1)S(1)} %all-to-all-done.refs_2_, ...), custom_call_target="tpu_custom_call" | custom-call | flops 1000000000 | bytes 2000000 | tf_op jit(solution)/shard_map/pallas_call | solution.py:203
  60.6 1.2 %collective-permute-start.16 = (bf16[4,2,128,128]{3,2,1,0:T(8,128)(2,1)S(1)}, bf16[4,2,128,128]{3,2,1,0:T(8,128)(2,1)S(1)}, u32[]{:S(2)}, u32[]{:S(2)}) collective-permute-start(bf16[4,2,128,128]{3,2,1,0:T(8,128)(2,1)S(1)} %add_convert_fusion.1), channel_id=1, source_target_pairs={{0,28},{1,5},{2,30},{3,7},{4,0},{5,9},{6,2},{7,11},{8,4},{9,13},{1... | collective-permute-start | bytes 786440 | tf_op jit(solution)/shard_map/ppermute | solution.py:253
  61.8 3.7 %all-to-all-start.1 = ((bf16[8,2,128,128]{3,2,1,0:T(8,128)(2,1)}), bf16[8,2,128,128]{3,2,1,0:T(8,128)(2,1)S(1)}, u32[]{:S(2)}, u32[]{:S(2)}) async-start(bf16[8,2,128,128]{3,2,1,0:T(8,128)(2,1)} %get-tuple-element.80), calls=%async_computation.1 | async-start | bytes 1048576 | tf_op jit(solution)/shard_map/all_to_all | solution.py:307
  65.5 1.4 %collective-permute-start.13 = (bf16[2,2,128,128]{3,2,1,0:T(8,128)(2,1)S(1)}, bf16[2,2,128,128]{3,2,1,0:T(8,128)(2,1)S(1)}, u32[]{:S(2)}, u32[]{:S(2)}) collective-permute-start(bf16[2,2,128,128]{3,2,1,0:T(8,128)(2,1)S(1)} %slice.34), channel_id=1, source_target_pairs={{0,2},{1,3},{2,0},{3,1},{4,6},{5,7},{6,4},{7,5},{8,10},{9,11},{10,... | collective-permute-start | bytes 393224 | tf_op jit(solution)/shard_map/ppermute | solution.py:253
  67.7 2.8 %collective-permute-start.17 = (bf16[2,2,128,128]{3,2,1,0:T(8,128)(2,1)S(1)}, bf16[2,2,128,128]{3,2,1,0:T(8,128)(2,1)S(1)}, u32[]{:S(2)}, u32[]{:S(2)}) collective-permute-start(bf16[2,2,128,128]{3,2,1,0:T(8,128)(2,1)S(1)} %get-tuple-element.94), channel_id=1, source_target_pairs={{0,28},{1,7},{2,30},{3,5},{4,0},{5,11},{6,2},{7,9},{8,4},{9,15},{1... | collective-permute-start | bytes 393224 | tf_op jit(solution)/shard_map/ppermute | solution.py:253
  70.5 3.0 %collective-permute-start.18 = (bf16[2,2,128,128]{3,2,1,0:T(8,128)(2,1)S(1)}, bf16[2,2,128,128]{3,2,1,0:T(8,128)(2,1)S(1)}, u32[]{:S(2)}, u32[]{:S(2)}) collective-permute-start(bf16[2,2,128,128]{3,2,1,0:T(8,128)(2,1)S(1)} %get-tuple-element.95), channel_id=1, source_target_pairs={{0,30},{1,5},{2,28},{3,7},{4,2},{5,9},{6,0},{7,11},{8,6},{9,13},{1... | collective-permute-start | bytes 393224 | tf_op jit(solution)/shard_map/ppermute | solution.py:253
  73.5 5.8 %collective-permute-done.13 = bf16[2,2,128,128]{3,2,1,0:T(8,128)(2,1)S(1)} collective-permute-done((bf16[2,2,128,128]{3,2,1,0:T(8,128)(2,1)S(1)}, bf16[2,2,128,128]{3,2,1,0:T(8,128)(2,1)S(1)}, u32[]{:S(2)}, u32[]{:S(2)}) %collective-permute-start.13) | collective-permute-done | bytes 131104 | tf_op jit(solution)/shard_map/ppermute | solution.py:253
  79.8 1.2 %collective-permute-start.19 = (bf16[2,128,128]{2,1,0:T(8,128)(2,1)S(1)}, bf16[2,128,128]{2,1,0:T(8,128)(2,1)S(1)}, u32[]{:S(2)}, u32[]{:S(2)}) collective-permute-start(bf16[2,128,128]{2,1,0:T(8,128)(2,1)S(1)} %fusion.1), channel_id=1, source_target_pairs={{0,1},{1,0},{2,3},{3,2},{4,5},{5,4},{6,7},{7,6},{8,9},{9,8},{10,11... | collective-permute-start | bytes 196616 | tf_op jit(solution)/shard_map/ppermute | solution.py:253
  (63 shorter events, 15.4 us)
Async XLA Ops:
  0.6 11.6 %copy-start.1 = (bf16[128,1024]{1,0:T(8,128)(2,1)S(1)}, bf16[128,1024]{1,0:T(8,128)(2,1)}, u32[]{:S(2)}) copy-start(bf16[128,1024]{1,0:T(8,128)(2,1)} %param.6) | copy-start | bytes 786436
  1.5 4.2 %collective-permute-start = (bf16[2,128,128]{2,1,0:T(8,128)(2,1)S(1)}, bf16[2,128,128]{2,1,0:T(8,128)(2,1)S(1)}, u32[]{:S(2)}, u32[]{:S(2)}) collective-permute-start(bf16[2,128,128]{2,1,0:T(8,128)(2,1)S(1)} %get-tuple-element.99), channel_id=1, source_target_pairs={{0,1},{1,0},{2,3},{3,2},{4,5},{5,4},{6,7},{7,6},{8,9},{9,8},{10,11... | collective-permute-start | bytes 196616 | tf_op jit(solution)/shard_map/ppermute | solution.py:253
  5.7 13.8 %collective-permute-start.1 = (bf16[2,2,128,128]{3,2,1,0:T(8,128)(2,1)S(1)}, bf16[2,2,128,128]{3,2,1,0:T(8,128)(2,1)S(1)}, u32[]{:S(2)}, u32[]{:S(2)}) collective-permute-start(bf16[2,2,128,128]{3,2,1,0:T(8,128)(2,1)S(1)} %pad_maximum_fusion.1), channel_id=1, source_target_pairs={{0,4},{1,31},{2,6},{3,29},{4,8},{5,3},{6,10},{7,1},{8,12},{9,7},{1... | collective-permute-start | bytes 393224 | tf_op jit(solution)/shard_map/ppermute | solution.py:253
  13.8 5.8 %collective-permute-start.2 = (bf16[2,2,128,128]{3,2,1,0:T(8,128)(2,1)S(1)}, bf16[2,2,128,128]{3,2,1,0:T(8,128)(2,1)S(1)}, u32[]{:S(2)}, u32[]{:S(2)}) collective-permute-start(bf16[2,2,128,128]{3,2,1,0:T(8,128)(2,1)S(1)} %pad_maximum_fusion.1), channel_id=1, source_target_pairs={{0,6},{1,29},{2,4},{3,31},{4,10},{5,1},{6,8},{7,3},{8,14},{9,5},{1... | collective-permute-start | bytes 393224 | tf_op jit(solution)/shard_map/ppermute | solution.py:253
  15.4 12.8 %all-to-all-start = ((bf16[8,2,128,128]{3,2,1,0:T(8,128)(2,1)}), bf16[8,2,128,128]{3,2,1,0:T(8,128)(2,1)S(1)}, u32[]{:S(2)}, u32[]{:S(2)}) async-start(bf16[8,2,128,128]{3,2,1,0:T(8,128)(2,1)} %maximum_bitcast_fusion), calls=%async_computation | async-start | bytes 1048576 | tf_op jit(solution)/shard_map/all_to_all | solution.py:275
  19.6 9.7 %copy-start.3 = (s32[4096]{0:T(1024)S(1)}, s32[4096]{0:T(1024)}, u32[]{:S(2)}) copy-start(s32[4096]{0:T(1024)} %param.11) | copy-start | bytes 49156
  19.6 8.6 %collective-permute-start.3 = (bf16[4,2,128,128]{3,2,1,0:T(8,128)(2,1)S(1)}, bf16[4,2,128,128]{3,2,1,0:T(8,128)(2,1)S(1)}, u32[]{:S(2)}, u32[]{:S(2)}) collective-permute-start(bf16[4,2,128,128]{3,2,1,0:T(8,128)(2,1)S(1)} %constant_dynamic-update-slice_fusion.refs_3_.refs_4_), channel_id=1, source_target_pairs={{0,4},{1,29},{2,6},{3,31},{4,8},{5,1},{6,10},{7,3},{8,12},{9,5},{1... | collective-permute-start | bytes 786440 | tf_op jit(solution)/shard_map/ppermute | solution.py:253
  20.4 16.6 %collective-permute-start.9 = (bf16[2,2,128,128]{3,2,1,0:T(8,128)(2,1)S(1)}, bf16[2,2,128,128]{3,2,1,0:T(8,128)(2,1)S(1)}, u32[]{:S(2)}, u32[]{:S(2)}) collective-permute-start(bf16[2,2,128,128]{3,2,1,0:T(8,128)(2,1)S(1)} %pad_maximum_fusion.1), channel_id=1, source_target_pairs={{0,2},{1,3},{2,0},{3,1},{4,6},{5,7},{6,4},{7,5},{8,10},{9,11},{10,... | collective-permute-start | bytes 393224 | tf_op jit(solution)/shard_map/ppermute | solution.py:253
  28.2 5.7 %collective-permute-start.4 = (bf16[4,2,128,128]{3,2,1,0:T(8,128)(2,1)S(1)}, bf16[4,2,128,128]{3,2,1,0:T(8,128)(2,1)S(1)}, u32[]{:S(2)}, u32[]{:S(2)}) collective-permute-start(bf16[4,2,128,128]{3,2,1,0:T(8,128)(2,1)S(1)} %collective-permute-done.3.refs_4_), channel_id=1, source_target_pairs={{0,4},{1,29},{2,6},{3,31},{4,8},{5,1},{6,10},{7,3},{8,12},{9,5},{1... | collective-permute-start | bytes 786440 | tf_op jit(solution)/shard_map/ppermute | solution.py:253
  33.9 5.5 %collective-permute-start.7 = (bf16[4,2,128,128]{3,2,1,0:T(8,128)(2,1)S(1)}, bf16[4,2,128,128]{3,2,1,0:T(8,128)(2,1)S(1)}, u32[]{:S(2)}, u32[]{:S(2)}) collective-permute-start(bf16[4,2,128,128]{3,2,1,0:T(8,128)(2,1)S(1)} %constant_dynamic-update-slice_fusion.refs_3_.refs_4_), channel_id=1, source_target_pairs={{0,1},{1,0},{2,3},{3,2},{4,5},{5,4},{6,7},{7,6},{8,9},{9,8},{10,11... | collective-permute-start | bytes 786440 | tf_op jit(solution)/shard_map/ppermute | solution.py:253
  35.2 4.2 %collective-permute-start.8 = (bf16[4,2,128,128]{3,2,1,0:T(8,128)(2,1)S(1)}, bf16[4,2,128,128]{3,2,1,0:T(8,128)(2,1)S(1)}, u32[]{:S(2)}, u32[]{:S(2)}) collective-permute-start(bf16[4,2,128,128]{3,2,1,0:T(8,128)(2,1)S(1)} %collective-permute-done.3.refs_4_), channel_id=1, source_target_pairs={{0,1},{1,0},{2,3},{3,2},{4,5},{5,4},{6,7},{7,6},{8,9},{9,8},{10,11... | collective-permute-start | bytes 786440 | tf_op jit(solution)/shard_map/ppermute | solution.py:253
  35.2 6.1 %collective-permute-start.6 = (bf16[4,2,128,128]{3,2,1,0:T(8,128)(2,1)S(1)}, bf16[4,2,128,128]{3,2,1,0:T(8,128)(2,1)S(1)}, u32[]{:S(2)}, u32[]{:S(2)}) collective-permute-start(bf16[4,2,128,128]{3,2,1,0:T(8,128)(2,1)S(1)} %collective-permute-done.4.refs_3_.refs_4_), channel_id=1, source_target_pairs={{0,4},{1,29},{2,6},{3,31},{4,8},{5,1},{6,10},{7,3},{8,12},{9,5},{1... | collective-permute-start | bytes 786440 | tf_op jit(solution)/shard_map/ppermute | solution.py:253
  36.2 5.1 %collective-permute-start.5 = (bf16[4,2,128,128]{3,2,1,0:T(8,128)(2,1)S(1)}, bf16[4,2,128,128]{3,2,1,0:T(8,128)(2,1)S(1)}, u32[]{:S(2)}, u32[]{:S(2)}) collective-permute-start(bf16[4,2,128,128]{3,2,1,0:T(8,128)(2,1)S(1)} %collective-permute-done.4.refs_3_.refs_4_), channel_id=1, source_target_pairs={{0,1},{1,0},{2,3},{3,2},{4,5},{5,4},{6,7},{7,6},{8,9},{9,8},{10,11... | collective-permute-start | bytes 786440 | tf_op jit(solution)/shard_map/ppermute | solution.py:253
  45.5 7.6 %collective-permute-start.11 = (bf16[4,2,128,128]{3,2,1,0:T(8,128)(2,1)S(1)}, bf16[4,2,128,128]{3,2,1,0:T(8,128)(2,1)S(1)}, u32[]{:S(2)}, u32[]{:S(2)}) collective-permute-start(bf16[4,2,128,128]{3,2,1,0:T(8,128)(2,1)S(1)} %get-tuple-element.64), channel_id=1, source_target_pairs={{0,28},{1,5},{2,30},{3,7},{4,0},{5,9},{6,2},{7,11},{8,4},{9,13},{1... | collective-permute-start | bytes 786440 | tf_op jit(solution)/shard_map/ppermute | solution.py:253
  46.1 7.1 %collective-permute-start.10 = (bf16[4,2,128,128]{3,2,1,0:T(8,128)(2,1)S(1)}, bf16[4,2,128,128]{3,2,1,0:T(8,128)(2,1)S(1)}, u32[]{:S(2)}, u32[]{:S(2)}) collective-permute-start(bf16[4,2,128,128]{3,2,1,0:T(8,128)(2,1)S(1)} %get-tuple-element.63), channel_id=1, source_target_pairs={{0,1},{1,0},{2,3},{3,2},{4,5},{5,4},{6,7},{7,6},{8,9},{9,8},{10,11... | collective-permute-start | bytes 786440 | tf_op jit(solution)/shard_map/ppermute | solution.py:253
  53.3 6.5 %collective-permute-start.12 = (bf16[4,2,128,128]{3,2,1,0:T(8,128)(2,1)S(1)}, bf16[4,2,128,128]{3,2,1,0:T(8,128)(2,1)S(1)}, u32[]{:S(2)}, u32[]{:S(2)}) collective-permute-start(bf16[4,2,128,128]{3,2,1,0:T(8,128)(2,1)S(1)} %add_convert_fusion.2), channel_id=1, source_target_pairs={{0,28},{1,5},{2,30},{3,7},{4,0},{5,9},{6,2},{7,11},{8,4},{9,13},{1... | collective-permute-start | bytes 786440 | tf_op jit(solution)/shard_map/ppermute | solution.py:253
  53.4 7.2 %collective-permute-start.15 = (bf16[4,2,128,128]{3,2,1,0:T(8,128)(2,1)S(1)}, bf16[4,2,128,128]{3,2,1,0:T(8,128)(2,1)S(1)}, u32[]{:S(2)}, u32[]{:S(2)}) collective-permute-start(bf16[4,2,128,128]{3,2,1,0:T(8,128)(2,1)S(1)} %get-tuple-element.78), channel_id=1, source_target_pairs={{0,1},{1,0},{2,3},{3,2},{4,5},{5,4},{6,7},{7,6},{8,9},{9,8},{10,11... | collective-permute-start | bytes 786440 | tf_op jit(solution)/shard_map/ppermute | solution.py:253
  59.8 7.1 %collective-permute-start.14 = (bf16[4,2,128,128]{3,2,1,0:T(8,128)(2,1)S(1)}, bf16[4,2,128,128]{3,2,1,0:T(8,128)(2,1)S(1)}, u32[]{:S(2)}, u32[]{:S(2)}) collective-permute-start(bf16[4,2,128,128]{3,2,1,0:T(8,128)(2,1)S(1)} %get-tuple-element.76), channel_id=1, source_target_pairs={{0,1},{1,0},{2,3},{3,2},{4,5},{5,4},{6,7},{7,6},{8,9},{9,8},{10,11... | collective-permute-start | bytes 786440 | tf_op jit(solution)/shard_map/ppermute | solution.py:253
  60.6 7.0 %collective-permute-start.16 = (bf16[4,2,128,128]{3,2,1,0:T(8,128)(2,1)S(1)}, bf16[4,2,128,128]{3,2,1,0:T(8,128)(2,1)S(1)}, u32[]{:S(2)}, u32[]{:S(2)}) collective-permute-start(bf16[4,2,128,128]{3,2,1,0:T(8,128)(2,1)S(1)} %add_convert_fusion.1), channel_id=1, source_target_pairs={{0,28},{1,5},{2,30},{3,7},{4,0},{5,9},{6,2},{7,11},{8,4},{9,13},{1... | collective-permute-start | bytes 786440 | tf_op jit(solution)/shard_map/ppermute | solution.py:253
  61.8 17.5 %all-to-all-start.1 = ((bf16[8,2,128,128]{3,2,1,0:T(8,128)(2,1)}), bf16[8,2,128,128]{3,2,1,0:T(8,128)(2,1)S(1)}, u32[]{:S(2)}, u32[]{:S(2)}) async-start(bf16[8,2,128,128]{3,2,1,0:T(8,128)(2,1)} %get-tuple-element.80), calls=%async_computation.1 | async-start | bytes 1048576 | tf_op jit(solution)/shard_map/all_to_all | solution.py:307
  65.5 13.8 %collective-permute-start.13 = (bf16[2,2,128,128]{3,2,1,0:T(8,128)(2,1)S(1)}, bf16[2,2,128,128]{3,2,1,0:T(8,128)(2,1)S(1)}, u32[]{:S(2)}, u32[]{:S(2)}) collective-permute-start(bf16[2,2,128,128]{3,2,1,0:T(8,128)(2,1)S(1)} %slice.34), channel_id=1, source_target_pairs={{0,2},{1,3},{2,0},{3,1},{4,6},{5,7},{6,4},{7,5},{8,10},{9,11},{10,... | collective-permute-start | bytes 393224 | tf_op jit(solution)/shard_map/ppermute | solution.py:253
  67.7 11.5 %collective-permute-start.17 = (bf16[2,2,128,128]{3,2,1,0:T(8,128)(2,1)S(1)}, bf16[2,2,128,128]{3,2,1,0:T(8,128)(2,1)S(1)}, u32[]{:S(2)}, u32[]{:S(2)}) collective-permute-start(bf16[2,2,128,128]{3,2,1,0:T(8,128)(2,1)S(1)} %get-tuple-element.94), channel_id=1, source_target_pairs={{0,28},{1,7},{2,30},{3,5},{4,0},{5,11},{6,2},{7,9},{8,4},{9,15},{1... | collective-permute-start | bytes 393224 | tf_op jit(solution)/shard_map/ppermute | solution.py:253
  70.5 8.8 %collective-permute-start.18 = (bf16[2,2,128,128]{3,2,1,0:T(8,128)(2,1)S(1)}, bf16[2,2,128,128]{3,2,1,0:T(8,128)(2,1)S(1)}, u32[]{:S(2)}, u32[]{:S(2)}) collective-permute-start(bf16[2,2,128,128]{3,2,1,0:T(8,128)(2,1)S(1)} %get-tuple-element.95), channel_id=1, source_target_pairs={{0,30},{1,5},{2,28},{3,7},{4,2},{5,9},{6,0},{7,11},{8,6},{9,13},{1... | collective-permute-start | bytes 393224 | tf_op jit(solution)/shard_map/ppermute | solution.py:253
  79.8 2.9 %collective-permute-start.19 = (bf16[2,128,128]{2,1,0:T(8,128)(2,1)S(1)}, bf16[2,128,128]{2,1,0:T(8,128)(2,1)S(1)}, u32[]{:S(2)}, u32[]{:S(2)}) collective-permute-start(bf16[2,128,128]{2,1,0:T(8,128)(2,1)S(1)} %fusion.1), channel_id=1, source_target_pairs={{0,1},{1,0},{2,3},{3,2},{4,5},{5,4},{6,7},{7,6},{8,9},{9,8},{10,11... | collective-permute-start | bytes 196616 | tf_op jit(solution)/shard_map/ppermute | solution.py:253
  (2 other events, 1.6 us)

commit v4 on v3

--- a/solution.py
+++ b/solution.py
@@ -230,6 +230,28 @@
     return call(functools.partial(backward_kernel, kinds, first, last), operands, outs, scratch, 10**9)
 
 
+def split_heads(q, do, both):
+    for i in range(GROUP):
+        both[i, 0] = q[:, i * HEAD : (i + 1) * HEAD]
+        both[i, 1] = do[:, i * HEAD : (i + 1) * HEAD]
+
+
+def join_heads(both, out, dq):
+    for i in range(GROUP):
+        out[:, i * HEAD : (i + 1) * HEAD] = both[i, 0]
+        dq[:, i * HEAD : (i + 1) * HEAD] = both[i, 1]
+
+
+def relayout(kernel, operands, outs):
+    return pl.pallas_call(
+        kernel,
+        out_shape=[jax.ShapeDtypeStruct(shape, BF16) for shape in outs],
+        in_specs=[VMEM] * len(operands),
+        out_specs=[VMEM] * len(outs),
+        cost_estimate=pl.CostEstimate(flops=0, bytes_accessed=10**6, transcendentals=0),
+    )(*operands)
+
+
 def outer_perm(move):
     pairs = []
     for z in range(8):
@@ -271,8 +293,8 @@
     pair = jnp.stack([kv, send(kv, CORE)])
     near1 = jnp.concatenate([send(pair, pairs) for pairs in FIRST_ON])
     own = jnp.concatenate([pair, send(pair, TWIN)])
-    qd = jnp.stack([queries.reshape(rows, GROUP, HEAD), output_gradient.reshape(rows, GROUP, HEAD)])
-    qd = lax.all_to_all(jnp.transpose(qd, (2, 0, 1, 3)), "head", 0, 0, tiled=True)
+    (qd,) = relayout(split_heads, [queries, output_gradient], [(GROUP, 2, rows, HEAD)])
+    qd = lax.all_to_all(qd, "head", 0, 0, tiled=True)
     segment_ids, qd = after(segment_ids, qd)
     starts = jnp.sum(segment_ids[None, :] < jnp.arange(1, 4, dtype=jnp.int32)[:, None], axis=1)
     place = jnp.stack([lax.axis_index("inner"), lax.axis_index("outer")])
@@ -306,9 +328,9 @@
     own_twin = send(own[2:], TWIN)
     back = lax.all_to_all(back, "head", 0, 0, tiled=True)
     moving = add(near1, far1, moving)
+    attended, query_grad = relayout(join_heads, [back], [(rows, GROUP * HEAD)] * 2)
+    own_twin, attended, query_grad = after(own_twin, attended, query_grad)
     pair = total32(own[:2], own_twin, *(send(moving[2 * n : 2 * n + 2], LAST_HOME[n]) for n in range(2)))
-    back = jnp.transpose(back, (1, 2, 0, 3)).reshape(2, rows, GROUP * HEAD)
-    pair, attended, query_grad = after(pair, back[0], back[1])
     total = add(pair[0], send(pair[1].astype(BF16), CORE))
     return attended, query_grad, total[0], total[1]
 

time: 84.3 us -> 81.8 us (0.970)
  local copies, waits for them, and re-layouts: 4.84 us -> 2.08 us
  Pallas kernels: 17.6 us -> 20 us
  waiting for transfers between devices: 16.2 us -> 15 us
  other arithmetic: 2.41 us -> 1.53 us
    pallas_call x0 -> x2, Pallas kernels: none -> 3.89 us  [relayout(): pl.pallas_call(kernel, out_shape=[jax.ShapeDtypeStruct(shape, BF16) for s...]
    unnamed x13 -> x7, local copies, waits for them, and re-layouts: 3.39 us -> 1.39 us
    pallas_call x8, Pallas kernels: 17.6 us -> 16.1 us  [call(): pl.pallas_call(kernel, out_shape=outs, in_specs=[SMEM, SMEM] + [VMEM] * (...]
    ppermute x20, waiting for transfers between devices: 10 us -> 8.72 us  [send(): return lax.ppermute(x, AXES, pairs)]
  transfers between devices with their start and end apart: 22 -> 22, of which waited for: 6 -> 7; matrix products, arithmetic and copies ran while one was open for 5% -> 1% of each run, Pallas kernels for 16% -> 19%
where the time goes in v4:
time: 81.8 us; the launch traced here: 81.3 us
  starting transfers between devices  41.9 us (51%)
  Pallas kernels  20 us (24%)
  waiting for transfers between devices  15 us (18%)
  local copies, waits for them, and re-layouts  2.08 us (3%)
  other arithmetic  1.53 us (2%)
  between operations  0.84 us (1%)
    ppermute x20, starting transfers between devices, send(): return lax.ppermute(x, AXES, pairs)  33.6 us
    pallas_call x8, Pallas kernels, call(): pl.pallas_call(kernel, out_shape=outs, in_specs=[SMEM, SMEM] + [VMEM] * (...  16.1 us
    ppermute x20, waiting for transfers between devices, send(): return lax.ppermute(x, AXES, pairs)  8.72 us
    all_to_all x1, waiting for transfers between devices, on_device(): qd = lax.all_to_all(qd, 'head', 0, 0, tiled=True)  6.21 us
    all_to_all x1, starting transfers between devices, on_device(): back = lax.all_to_all(back, 'head', 0, 0, tiled=True)  4.18 us
    all_to_all x1, starting transfers between devices, on_device(): qd = lax.all_to_all(qd, 'head', 0, 0, tiled=True)  4.13 us
    pallas_call x2, Pallas kernels, relayout(): pl.pallas_call(kernel, out_shape=[jax.ShapeDtypeStruct(shape, BF16) for s...  3.89 us
  transfers between devices with their start and end apart: 22, of which 7 were waited for; matrix products, arithmetic and copies ran while one was open for 1% of the time, Pallas kernels for 19%

profile of v4, /device:TPU:1, one launch (start us, length us, event | category | flops | bytes accessed | tf_op | source)
XLA Modules:
  0.0 81.3 jit_solution(10192064523912580792)
XLA Ops:
  1.4 3.3 %collective-permute-start = (bf16[2,128,128]{2,1,0:T(8,128)(2,1)S(1)}, bf16[2,128,128]{2,1,0:T(8,128)(2,1)S(1)}, u32[]{:S(2)}, u32[]{:S(2)}) collective-permute-start(bf16[2,128,128]{2,1,0:T(8,128)(2,1)S(1)} %get-tuple-element.93), channel_id=1, source_target_pairs={{0,1},{1,0},{2,3},{3,2},{4,5},{5,4},{6,7},{7,6},{8,9},{9,8},{10,11... | collective-permute-start | bytes 196616 | tf_op jit(solution)/shard_map/ppermute | solution.py:275
  5.7 6.5 %collective-permute-start.1 = (bf16[2,2,128,128]{3,2,1,0:T(8,128)(2,1)S(1)}, bf16[2,2,128,128]{3,2,1,0:T(8,128)(2,1)S(1)}, u32[]{:S(2)}, u32[]{:S(2)}) collective-permute-start(bf16[2,2,128,128]{3,2,1,0:T(8,128)(2,1)S(1)} %pad_maximum_fusion.1), channel_id=1, source_target_pairs={{0,4},{1,31},{2,6},{3,29},{4,8},{5,3},{6,10},{7,1},{8,12},{9,7},{1... | collective-permute-start | bytes 393224 | tf_op jit(solution)/shard_map/ppermute | solution.py:275
  12.9 1.9 %shard_map.93 = bf16[8,2,128,128]{3,2,1,0:T(8,128)(2,1)} custom-call(bf16[128,1024]{1,0:T(8,128)(2,1)} %q.1, bf16[128,1024]{1,0:T(8,128)(2,1)} %do.1), custom_call_target="tpu_custom_call" | custom-call | bytes 1000000 | tf_op jit(solution)/shard_map/pallas_call | solution.py:246
  14.9 4.1 %all-to-all-start = ((bf16[8,2,128,128]{3,2,1,0:T(8,128)(2,1)}), bf16[8,2,128,128]{3,2,1,0:T(8,128)(2,1)S(1)}, u32[]{:S(2)}, u32[]{:S(2)}) async-start(bf16[8,2,128,128]{3,2,1,0:T(8,128)(2,1)} %shard_map.93), calls=%async_computation | async-start | bytes 1048576 | tf_op jit(solution)/shard_map/all_to_all | solution.py:297
  19.9 1.6 %collective-permute-start.9 = (bf16[2,2,128,128]{3,2,1,0:T(8,128)(2,1)S(1)}, bf16[2,2,128,128]{3,2,1,0:T(8,128)(2,1)S(1)}, u32[]{:S(2)}, u32[]{:S(2)}) collective-permute-start(bf16[2,2,128,128]{3,2,1,0:T(8,128)(2,1)S(1)} %pad_maximum_fusion.1), channel_id=1, source_target_pairs={{0,2},{1,3},{2,0},{3,1},{4,6},{5,7},{6,4},{7,5},{8,10},{9,11},{10,... | collective-permute-start | bytes 393224 | tf_op jit(solution)/shard_map/ppermute | solution.py:275
  21.4 6.2 %all-to-all-done.refs_2_ = bf16[8,2,128,128]{3,2,1,0:T(8,128)(2,1)S(1)} async-done(((bf16[8,2,128,128]{3,2,1,0:T(8,128)(2,1)}), bf16[8,2,128,128]{3,2,1,0:T(8,128)(2,1)S(1)}, u32[]{:S(2)}, u32[]{:S(2)}) %all-to-all-start) | async-done | bytes 524320 | tf_op jit(solution)/shard_map/all_to_all | solution.py:297
  29.6 1.8 %shard_map.94 = (f32[2,2,8,512]{3,2,1,0:T(8,128)S(1)}, f32[2,128,512]{2,1,0:T(8,128)S(1)}) custom-call(s32[64]{0:T(128)S(1)} %copy-done, s32[5]{0:T(128)S(1)} %pad_add_fusion.refs_1_, bf16[8,2,128,128]{3,2,1,0:T(8,128)(2,1)S(1)} %all-to-all-done.refs_2_, bf16[4,2,128,128]{3,2,1,0:T(8,128)(2,1)S(1)} %constant_dynamic-update-slice_fusion.refs_3_.refs_4_, ...), custom_call_target="tpu_custom_call" | custom-call | flops 500000000 | bytes 2000000 | tf_op jit(solution)/shard_map/pallas_call | solution.py:203
  31.4 2.0 %collective-permute-done.4.refs_3_.refs_4_ = bf16[4,2,128,128]{3,2,1,0:T(8,128)(2,1)S(1)} collective-permute-done((bf16[4,2,128,128]{3,2,1,0:T(8,128)(2,1)S(1)}, bf16[4,2,128,128]{3,2,1,0:T(8,128)(2,1)S(1)}, u32[]{:S(2)}, u32[]{:S(2)}) %collective-permute-start.4) | collective-permute-done | bytes 262176 | tf_op jit(solution)/shard_map/ppermute | solution.py:275
  36.5 1.8 %shard_map.95 = (f32[2,2,8,512]{3,2,1,0:T(8,128)S(1)}, f32[2,128,512]{2,1,0:T(8,128)S(1)}) custom-call(s32[64]{0:T(128)S(1)} %copy-done, s32[5]{0:T(128)S(1)} %pad_add_fusion.refs_1_, bf16[8,2,128,128]{3,2,1,0:T(8,128)(2,1)S(1)} %all-to-all-done.refs_2_, bf16[4,2,128,128]{3,2,1,0:T(8,128)(2,1)S(1)} %collective-permute-done.4.refs_3_.refs_4_, ...), custom_call_target="tpu_custom_call" | custom-call | flops 500000000 | bytes 2000000 | tf_op jit(solution)/shard_map/pallas_call | solution.py:203
  38.3 1.4 %shard_map.96 = (f32[2,2,8,512]{3,2,1,0:T(8,128)S(1)}, f32[2,128,512]{2,1,0:T(8,128)S(1)}) custom-call(s32[64]{0:T(128)S(1)} %copy-done, s32[5]{0:T(128)S(1)} %pad_add_fusion.refs_1_, bf16[8,2,128,128]{3,2,1,0:T(8,128)(2,1)S(1)} %all-to-all-done.refs_2_, bf16[4,2,128,128]{3,2,1,0:T(8,128)(2,1)S(1)} %collective-permute-done.7.refs_3_.refs_5_, ...), custom_call_target="tpu_custom_call" | custom-call | flops 500000000 | bytes 2000000 | tf_op jit(solution)/shard_map/pallas_call | solution.py:203
  40.1 2.0 %shard_map.97 = (f32[2,2,8,512]{3,2,1,0:T(8,128)S(1)}, bf16[8,128,128]{2,1,0:T(8,128)(2,1)S(1)}) custom-call(s32[64]{0:T(128)S(1)} %copy-done, s32[5]{0:T(128)S(1)} %pad_add_fusion.refs_1_, bf16[8,2,128,128]{3,2,1,0:T(8,128)(2,1)S(1)} %all-to-all-done.refs_2_, bf16[4,2,128,128]{3,2,1,0:T(8,128)(2,1)S(1)} %collective-permute-done.5.refs_3_.refs_4_, ...), custom_call_target="tpu_custom_call" | custom-call | flops 500000000 | bytes 2000000 | tf_op jit(solution)/shard_map/pallas_call | solution.py:203
  42.2 2.2 %shard_map.98 = (bf16[4,2,128,128]{3,2,1,0:T(8,128)(2,1)S(1)}, bf16[4,2,128,128]{3,2,1,0:T(8,128)(2,1)S(1)}, f32[2,128,512]{2,1,0:T(8,128)S(1)}) custom-call(s32[64]{0:T(128)S(1)} %copy-done, s32[5]{0:T(128)S(1)} %pad_add_fusion.refs_1_, bf16[8,2,128,128]{3,2,1,0:T(8,128)(2,1)S(1)} %all-to-all-done.refs_2_, f32[2,2,8,512]{3,2,1,0:T(8,128)S(1)} %get-tuple-element.62.refs_3_, ...), custom_call_target="tpu_custom_call" | custom-call | flops 1000000000 | bytes 2000000 | tf_op jit(solution)/shard_map/pallas_call | solution.py:203
  45.5 1.9 %collective-permute-start.10 = (bf16[4,2,128,128]{3,2,1,0:T(8,128)(2,1)S(1)}, bf16[4,2,128,128]{3,2,1,0:T(8,128)(2,1)S(1)}, u32[]{:S(2)}, u32[]{:S(2)}) collective-permute-start(bf16[4,2,128,128]{3,2,1,0:T(8,128)(2,1)S(1)} %get-tuple-element.65), channel_id=1, source_target_pairs={{0,1},{1,0},{2,3},{3,2},{4,5},{5,4},{6,7},{7,6},{8,9},{9,8},{10,11... | collective-permute-start | bytes 786440 | tf_op jit(solution)/shard_map/ppermute | solution.py:275
  47.4 2.0 %shard_map.99 = (bf16[4,2,128,128]{3,2,1,0:T(8,128)(2,1)S(1)}, bf16[4,2,128,128]{3,2,1,0:T(8,128)(2,1)S(1)}, f32[2,128,512]{2,1,0:T(8,128)S(1)}) custom-call(s32[64]{0:T(128)S(1)} %copy-done, s32[5]{0:T(128)S(1)} %pad_add_fusion.refs_1_, bf16[8,2,128,128]{3,2,1,0:T(8,128)(2,1)S(1)} %all-to-all-done.refs_2_, f32[2,2,8,512]{3,2,1,0:T(8,128)S(1)} %get-tuple-element.62.refs_3_, ...), custom_call_target="tpu_custom_call" | custom-call | flops 1000000000 | bytes 2000000 | tf_op jit(solution)/shard_map/pallas_call | solution.py:203
  49.4 2.0 %shard_map.100 = (bf16[4,2,128,128]{3,2,1,0:T(8,128)(2,1)S(1)}, bf16[4,2,128,128]{3,2,1,0:T(8,128)(2,1)S(1)}, f32[2,128,512]{2,1,0:T(8,128)S(1)}) custom-call(s32[64]{0:T(128)S(1)} %copy-done, s32[5]{0:T(128)S(1)} %pad_add_fusion.refs_1_, bf16[8,2,128,128]{3,2,1,0:T(8,128)(2,1)S(1)} %all-to-all-done.refs_2_, f32[2,2,8,512]{3,2,1,0:T(8,128)S(1)} %get-tuple-element.62.refs_3_, ...), custom_call_target="tpu_custom_call" | custom-call | flops 1000000000 | bytes 2000000 | tf_op jit(solution)/shard_map/pallas_call | solution.py:203
  52.5 2.7 %collective-permute-start.15 = (bf16[4,2,128,128]{3,2,1,0:T(8,128)(2,1)S(1)}, bf16[4,2,128,128]{3,2,1,0:T(8,128)(2,1)S(1)}, u32[]{:S(2)}, u32[]{:S(2)}) collective-permute-start(bf16[4,2,128,128]{3,2,1,0:T(8,128)(2,1)S(1)} %get-tuple-element.86), channel_id=1, source_target_pairs={{0,1},{1,0},{2,3},{3,2},{4,5},{5,4},{6,7},{7,6},{8,9},{9,8},{10,11... | collective-permute-start | bytes 786440 | tf_op jit(solution)/shard_map/ppermute | solution.py:275
  55.2 2.8 %shard_map.101 = (bf16[4,2,128,128]{3,2,1,0:T(8,128)(2,1)S(1)}, bf16[4,2,128,128]{3,2,1,0:T(8,128)(2,1)S(1)}, bf16[8,2,128,128]{3,2,1,0:T(8,128)(2,1)}) custom-call(s32[64]{0:T(128)S(1)} %copy-done, s32[5]{0:T(128)S(1)} %pad_add_fusion.refs_1_, bf16[8,2,128,128]{3,2,1,0:T(8,128)(2,1)S(1)} %all-to-all-done.refs_2_, ...), custom_call_target="tpu_custom_call" | custom-call | flops 1000000000 | bytes 2000000 | tf_op jit(solution)/shard_map/pallas_call | solution.py:203
  58.1 1.9 %collective-permute-start.14 = (bf16[4,2,128,128]{3,2,1,0:T(8,128)(2,1)S(1)}, bf16[4,2,128,128]{3,2,1,0:T(8,128)(2,1)S(1)}, u32[]{:S(2)}, u32[]{:S(2)}) collective-permute-start(bf16[4,2,128,128]{3,2,1,0:T(8,128)(2,1)S(1)} %get-tuple-element.84), channel_id=1, source_target_pairs={{0,1},{1,0},{2,3},{3,2},{4,5},{5,4},{6,7},{7,6},{8,9},{9,8},{10,11... | collective-permute-start | bytes 786440 | tf_op jit(solution)/shard_map/ppermute | solution.py:275
  60.2 4.2 %all-to-all-start.1 = ((bf16[8,2,128,128]{3,2,1,0:T(8,128)(2,1)}), bf16[8,2,128,128]{3,2,1,0:T(8,128)(2,1)S(1)}, u32[]{:S(2)}, u32[]{:S(2)}) async-start(bf16[8,2,128,128]{3,2,1,0:T(8,128)(2,1)} %get-tuple-element.77), calls=%async_computation.1 | async-start | bytes 1048576 | tf_op jit(solution)/shard_map/all_to_all | solution.py:329
  64.4 1.8 %collective-permute-start.13 = (bf16[2,2,128,128]{3,2,1,0:T(8,128)(2,1)S(1)}, bf16[2,2,128,128]{3,2,1,0:T(8,128)(2,1)S(1)}, u32[]{:S(2)}, u32[]{:S(2)}) collective-permute-start(bf16[2,2,128,128]{3,2,1,0:T(8,128)(2,1)S(1)} %slice.25), channel_id=1, source_target_pairs={{0,2},{1,3},{2,0},{3,1},{4,6},{5,7},{6,4},{7,5},{8,10},{9,11},{10,... | collective-permute-start | bytes 393224 | tf_op jit(solution)/shard_map/ppermute | solution.py:275
  66.7 2.4 %collective-permute-start.17 = (bf16[2,2,128,128]{3,2,1,0:T(8,128)(2,1)S(1)}, bf16[2,2,128,128]{3,2,1,0:T(8,128)(2,1)S(1)}, u32[]{:S(2)}, u32[]{:S(2)}) collective-permute-start(bf16[2,2,128,128]{3,2,1,0:T(8,128)(2,1)S(1)} %get-tuple-element.88), channel_id=1, source_target_pairs={{0,28},{1,7},{2,30},{3,5},{4,0},{5,11},{6,2},{7,9},{8,4},{9,15},{1... | collective-permute-start | bytes 393224 | tf_op jit(solution)/shard_map/ppermute | solution.py:275
  69.1 2.3 %collective-permute-start.18 = (bf16[2,2,128,128]{3,2,1,0:T(8,128)(2,1)S(1)}, bf16[2,2,128,128]{3,2,1,0:T(8,128)(2,1)S(1)}, u32[]{:S(2)}, u32[]{:S(2)}) collective-permute-start(bf16[2,2,128,128]{3,2,1,0:T(8,128)(2,1)S(1)} %get-tuple-element.89), channel_id=1, source_target_pairs={{0,30},{1,5},{2,28},{3,7},{4,2},{5,9},{6,0},{7,11},{8,6},{9,13},{1... | collective-permute-start | bytes 393224 | tf_op jit(solution)/shard_map/ppermute | solution.py:275
  72.3 2.0 %shard_map.102 = (bf16[128,1024]{1,0:T(8,128)(2,1)}, bf16[128,1024]{1,0:T(8,128)(2,1)}) custom-call(bf16[8,2,128,128]{3,2,1,0:T(8,128)(2,1)} %copy-done.1), custom_call_target="tpu_custom_call" | custom-call | bytes 1000000 | tf_op jit(solution)/shard_map/pallas_call | solution.py:246
  74.3 4.1 %collective-permute-done.13 = bf16[2,2,128,128]{3,2,1,0:T(8,128)(2,1)S(1)} collective-permute-done((bf16[2,2,128,128]{3,2,1,0:T(8,128)(2,1)S(1)}, bf16[2,2,128,128]{3,2,1,0:T(8,128)(2,1)S(1)}, u32[]{:S(2)}, u32[]{:S(2)}) %collective-permute-start.13) | collective-permute-done | bytes 131104 | tf_op jit(solution)/shard_map/ppermute | solution.py:275
  (53 shorter events, 15.4 us)
Async XLA Ops:
  1.4 4.2 %collective-permute-start = (bf16[2,128,128]{2,1,0:T(8,128)(2,1)S(1)}, bf16[2,128,128]{2,1,0:T(8,128)(2,1)S(1)}, u32[]{:S(2)}, u32[]{:S(2)}) collective-permute-start(bf16[2,128,128]{2,1,0:T(8,128)(2,1)S(1)} %get-tuple-element.93), channel_id=1, source_target_pairs={{0,1},{1,0},{2,3},{3,2},{4,5},{5,4},{6,7},{7,6},{8,9},{9,8},{10,11... | collective-permute-start | bytes 196616 | tf_op jit(solution)/shard_map/ppermute | solution.py:275
  5.7 13.3 %collective-permute-start.1 = (bf16[2,2,128,128]{3,2,1,0:T(8,128)(2,1)S(1)}, bf16[2,2,128,128]{3,2,1,0:T(8,128)(2,1)S(1)}, u32[]{:S(2)}, u32[]{:S(2)}) collective-permute-start(bf16[2,2,128,128]{3,2,1,0:T(8,128)(2,1)S(1)} %pad_maximum_fusion.1), channel_id=1, source_target_pairs={{0,4},{1,31},{2,6},{3,29},{4,8},{5,3},{6,10},{7,1},{8,12},{9,7},{1... | collective-permute-start | bytes 393224 | tf_op jit(solution)/shard_map/ppermute | solution.py:275
  12.2 6.8 %collective-permute-start.2 = (bf16[2,2,128,128]{3,2,1,0:T(8,128)(2,1)S(1)}, bf16[2,2,128,128]{3,2,1,0:T(8,128)(2,1)S(1)}, u32[]{:S(2)}, u32[]{:S(2)}) collective-permute-start(bf16[2,2,128,128]{3,2,1,0:T(8,128)(2,1)S(1)} %pad_maximum_fusion.1), channel_id=1, source_target_pairs={{0,6},{1,29},{2,4},{3,31},{4,10},{5,1},{6,8},{7,3},{8,14},{9,5},{1... | collective-permute-start | bytes 393224 | tf_op jit(solution)/shard_map/ppermute | solution.py:275
  14.9 12.8 %all-to-all-start = ((bf16[8,2,128,128]{3,2,1,0:T(8,128)(2,1)}), bf16[8,2,128,128]{3,2,1,0:T(8,128)(2,1)S(1)}, u32[]{:S(2)}, u32[]{:S(2)}) async-start(bf16[8,2,128,128]{3,2,1,0:T(8,128)(2,1)} %shard_map.93), calls=%async_computation | async-start | bytes 1048576 | tf_op jit(solution)/shard_map/all_to_all | solution.py:297
  19.0 9.7 %copy-start.2 = (s32[4096]{0:T(1024)S(1)}, s32[4096]{0:T(1024)}, u32[]{:S(2)}) copy-start(s32[4096]{0:T(1024)} %param.11) | copy-start | bytes 49156
  19.1 8.6 %collective-permute-start.3 = (bf16[4,2,128,128]{3,2,1,0:T(8,128)(2,1)S(1)}, bf16[4,2,128,128]{3,2,1,0:T(8,128)(2,1)S(1)}, u32[]{:S(2)}, u32[]{:S(2)}) collective-permute-start(bf16[4,2,128,128]{3,2,1,0:T(8,128)(2,1)S(1)} %constant_dynamic-update-slice_fusion.refs_3_.refs_4_), channel_id=1, source_target_pairs={{0,4},{1,29},{2,6},{3,31},{4,8},{5,1},{6,10},{7,3},{8,12},{9,5},{1... | collective-permute-start | bytes 786440 | tf_op jit(solution)/shard_map/ppermute | solution.py:275
  19.9 16.6 %collective-permute-start.9 = (bf16[2,2,128,128]{3,2,1,0:T(8,128)(2,1)S(1)}, bf16[2,2,128,128]{3,2,1,0:T(8,128)(2,1)S(1)}, u32[]{:S(2)}, u32[]{:S(2)}) collective-permute-start(bf16[2,2,128,128]{3,2,1,0:T(8,128)(2,1)S(1)} %pad_maximum_fusion.1), channel_id=1, source_target_pairs={{0,2},{1,3},{2,0},{3,1},{4,6},{5,7},{6,4},{7,5},{8,10},{9,11},{10,... | collective-permute-start | bytes 393224 | tf_op jit(solution)/shard_map/ppermute | solution.py:275
  27.7 5.7 %collective-permute-start.4 = (bf16[4,2,128,128]{3,2,1,0:T(8,128)(2,1)S(1)}, bf16[4,2,128,128]{3,2,1,0:T(8,128)(2,1)S(1)}, u32[]{:S(2)}, u32[]{:S(2)}) collective-permute-start(bf16[4,2,128,128]{3,2,1,0:T(8,128)(2,1)S(1)} %collective-permute-done.3.refs_4_), channel_id=1, source_target_pairs={{0,4},{1,29},{2,6},{3,31},{4,8},{5,1},{6,10},{7,3},{8,12},{9,5},{1... | collective-permute-start | bytes 786440 | tf_op jit(solution)/shard_map/ppermute | solution.py:275
  33.4 5.0 %collective-permute-start.7 = (bf16[4,2,128,128]{3,2,1,0:T(8,128)(2,1)S(1)}, bf16[4,2,128,128]{3,2,1,0:T(8,128)(2,1)S(1)}, u32[]{:S(2)}, u32[]{:S(2)}) collective-permute-start(bf16[4,2,128,128]{3,2,1,0:T(8,128)(2,1)S(1)} %constant_dynamic-update-slice_fusion.refs_3_.refs_4_), channel_id=1, source_target_pairs={{0,1},{1,0},{2,3},{3,2},{4,5},{5,4},{6,7},{7,6},{8,9},{9,8},{10,11... | collective-permute-start | bytes 786440 | tf_op jit(solution)/shard_map/ppermute | solution.py:275
  34.6 3.7 %collective-permute-start.8 = (bf16[4,2,128,128]{3,2,1,0:T(8,128)(2,1)S(1)}, bf16[4,2,128,128]{3,2,1,0:T(8,128)(2,1)S(1)}, u32[]{:S(2)}, u32[]{:S(2)}) collective-permute-start(bf16[4,2,128,128]{3,2,1,0:T(8,128)(2,1)S(1)} %collective-permute-done.3.refs_4_), channel_id=1, source_target_pairs={{0,1},{1,0},{2,3},{3,2},{4,5},{5,4},{6,7},{7,6},{8,9},{9,8},{10,11... | collective-permute-start | bytes 786440 | tf_op jit(solution)/shard_map/ppermute | solution.py:275
  34.6 5.5 %collective-permute-start.6 = (bf16[4,2,128,128]{3,2,1,0:T(8,128)(2,1)S(1)}, bf16[4,2,128,128]{3,2,1,0:T(8,128)(2,1)S(1)}, u32[]{:S(2)}, u32[]{:S(2)}) collective-permute-start(bf16[4,2,128,128]{3,2,1,0:T(8,128)(2,1)S(1)} %collective-permute-done.4.refs_3_.refs_4_), channel_id=1, source_target_pairs={{0,4},{1,29},{2,6},{3,31},{4,8},{5,1},{6,10},{7,3},{8,12},{9,5},{1... | collective-permute-start | bytes 786440 | tf_op jit(solution)/shard_map/ppermute | solution.py:275
  35.6 4.5 %collective-permute-start.5 = (bf16[4,2,128,128]{3,2,1,0:T(8,128)(2,1)S(1)}, bf16[4,2,128,128]{3,2,1,0:T(8,128)(2,1)S(1)}, u32[]{:S(2)}, u32[]{:S(2)}) collective-permute-start(bf16[4,2,128,128]{3,2,1,0:T(8,128)(2,1)S(1)} %collective-permute-done.4.refs_3_.refs_4_), channel_id=1, source_target_pairs={{0,1},{1,0},{2,3},{3,2},{4,5},{5,4},{6,7},{7,6},{8,9},{9,8},{10,11... | collective-permute-start | bytes 786440 | tf_op jit(solution)/shard_map/ppermute | solution.py:275
  44.4 7.1 %collective-permute-start.11 = (bf16[4,2,128,128]{3,2,1,0:T(8,128)(2,1)S(1)}, bf16[4,2,128,128]{3,2,1,0:T(8,128)(2,1)S(1)}, u32[]{:S(2)}, u32[]{:S(2)}) collective-permute-start(bf16[4,2,128,128]{3,2,1,0:T(8,128)(2,1)S(1)} %get-tuple-element.66), channel_id=1, source_target_pairs={{0,28},{1,5},{2,30},{3,7},{4,0},{5,9},{6,2},{7,11},{8,4},{9,13},{1... | collective-permute-start | bytes 786440 | tf_op jit(solution)/shard_map/ppermute | solution.py:275
  45.5 6.0 %collective-permute-start.10 = (bf16[4,2,128,128]{3,2,1,0:T(8,128)(2,1)S(1)}, bf16[4,2,128,128]{3,2,1,0:T(8,128)(2,1)S(1)}, u32[]{:S(2)}, u32[]{:S(2)}) collective-permute-start(bf16[4,2,128,128]{3,2,1,0:T(8,128)(2,1)S(1)} %get-tuple-element.65), channel_id=1, source_target_pairs={{0,1},{1,0},{2,3},{3,2},{4,5},{5,4},{6,7},{7,6},{8,9},{9,8},{10,11... | collective-permute-start | bytes 786440 | tf_op jit(solution)/shard_map/ppermute | solution.py:275
  51.6 6.5 %collective-permute-start.12 = (bf16[4,2,128,128]{3,2,1,0:T(8,128)(2,1)S(1)}, bf16[4,2,128,128]{3,2,1,0:T(8,128)(2,1)S(1)}, u32[]{:S(2)}, u32[]{:S(2)}) collective-permute-start(bf16[4,2,128,128]{3,2,1,0:T(8,128)(2,1)S(1)} %add_convert_fusion.2), channel_id=1, source_target_pairs={{0,28},{1,5},{2,30},{3,7},{4,0},{5,9},{6,2},{7,11},{8,4},{9,13},{1... | collective-permute-start | bytes 786440 | tf_op jit(solution)/shard_map/ppermute | solution.py:275
  52.5 7.5 %collective-permute-start.15 = (bf16[4,2,128,128]{3,2,1,0:T(8,128)(2,1)S(1)}, bf16[4,2,128,128]{3,2,1,0:T(8,128)(2,1)S(1)}, u32[]{:S(2)}, u32[]{:S(2)}) collective-permute-start(bf16[4,2,128,128]{3,2,1,0:T(8,128)(2,1)S(1)} %get-tuple-element.86), channel_id=1, source_target_pairs={{0,1},{1,0},{2,3},{3,2},{4,5},{5,4},{6,7},{7,6},{8,9},{9,8},{10,11... | collective-permute-start | bytes 786440 | tf_op jit(solution)/shard_map/ppermute | solution.py:275
  58.1 8.1 %collective-permute-start.14 = (bf16[4,2,128,128]{3,2,1,0:T(8,128)(2,1)S(1)}, bf16[4,2,128,128]{3,2,1,0:T(8,128)(2,1)S(1)}, u32[]{:S(2)}, u32[]{:S(2)}) collective-permute-start(bf16[4,2,128,128]{3,2,1,0:T(8,128)(2,1)S(1)} %get-tuple-element.84), channel_id=1, source_target_pairs={{0,1},{1,0},{2,3},{3,2},{4,5},{5,4},{6,7},{7,6},{8,9},{9,8},{10,11... | collective-permute-start | bytes 786440 | tf_op jit(solution)/shard_map/ppermute | solution.py:275
  60.1 6.5 %collective-permute-start.16 = (bf16[4,2,128,128]{3,2,1,0:T(8,128)(2,1)S(1)}, bf16[4,2,128,128]{3,2,1,0:T(8,128)(2,1)S(1)}, u32[]{:S(2)}, u32[]{:S(2)}) collective-permute-start(bf16[4,2,128,128]{3,2,1,0:T(8,128)(2,1)S(1)} %add_convert_fusion.1), channel_id=1, source_target_pairs={{0,28},{1,5},{2,30},{3,7},{4,0},{5,9},{6,2},{7,11},{8,4},{9,13},{1... | collective-permute-start | bytes 786440 | tf_op jit(solution)/shard_map/ppermute | solution.py:275
  60.2 11.3 %all-to-all-start.1 = ((bf16[8,2,128,128]{3,2,1,0:T(8,128)(2,1)}), bf16[8,2,128,128]{3,2,1,0:T(8,128)(2,1)S(1)}, u32[]{:S(2)}, u32[]{:S(2)}) async-start(bf16[8,2,128,128]{3,2,1,0:T(8,128)(2,1)} %get-tuple-element.77), calls=%async_computation.1 | async-start | bytes 1048576 | tf_op jit(solution)/shard_map/all_to_all | solution.py:329
  64.4 13.9 %collective-permute-start.13 = (bf16[2,2,128,128]{3,2,1,0:T(8,128)(2,1)S(1)}, bf16[2,2,128,128]{3,2,1,0:T(8,128)(2,1)S(1)}, u32[]{:S(2)}, u32[]{:S(2)}) collective-permute-start(bf16[2,2,128,128]{3,2,1,0:T(8,128)(2,1)S(1)} %slice.25), channel_id=1, source_target_pairs={{0,2},{1,3},{2,0},{3,1},{4,6},{5,7},{6,4},{7,5},{8,10},{9,11},{10,... | collective-permute-start | bytes 393224 | tf_op jit(solution)/shard_map/ppermute | solution.py:275
  66.7 11.6 %collective-permute-start.17 = (bf16[2,2,128,128]{3,2,1,0:T(8,128)(2,1)S(1)}, bf16[2,2,128,128]{3,2,1,0:T(8,128)(2,1)S(1)}, u32[]{:S(2)}, u32[]{:S(2)}) collective-permute-start(bf16[2,2,128,128]{3,2,1,0:T(8,128)(2,1)S(1)} %get-tuple-element.88), channel_id=1, source_target_pairs={{0,28},{1,7},{2,30},{3,5},{4,0},{5,11},{6,2},{7,9},{8,4},{9,15},{1... | collective-permute-start | bytes 393224 | tf_op jit(solution)/shard_map/ppermute | solution.py:275
  69.1 9.2 %collective-permute-start.18 = (bf16[2,2,128,128]{3,2,1,0:T(8,128)(2,1)S(1)}, bf16[2,2,128,128]{3,2,1,0:T(8,128)(2,1)S(1)}, u32[]{:S(2)}, u32[]{:S(2)}) collective-permute-start(bf16[2,2,128,128]{3,2,1,0:T(8,128)(2,1)S(1)} %get-tuple-element.89), channel_id=1, source_target_pairs={{0,30},{1,5},{2,28},{3,7},{4,2},{5,9},{6,0},{7,11},{8,6},{9,13},{1... | collective-permute-start | bytes 393224 | tf_op jit(solution)/shard_map/ppermute | solution.py:275
  71.5 0.8 copy-start.1
  78.4 2.2 %collective-permute-start.19 = (bf16[2,128,128]{2,1,0:T(8,128)(2,1)S(1)}, bf16[2,128,128]{2,1,0:T(8,128)(2,1)S(1)}, u32[]{:S(2)}, u32[]{:S(2)}) collective-permute-start(bf16[2,128,128]{2,1,0:T(8,128)(2,1)S(1)} %fusion.2), channel_id=1, source_target_pairs={{0,1},{1,0},{2,3},{3,2},{4,5},{5,4},{6,7},{7,6},{8,9},{9,8},{10,11... | collective-permute-start | bytes 196616 | tf_op jit(solution)/shard_map/ppermute | solution.py:275
  (1 other events, 0.7 us)
